TPU v7x, 512 devices: a whole 4x8x8 slice. The times are simulated.
512 devices in a mesh: leaf: 128 (over z, y, core), vec: 4 (over x).
Axes of the slice: x: 4, y: 8, z: 8, core: 2. Of those that a mesh axis runs over, the one named last changes fastest.
Arguments:
- vectors: bfloat16 [16, 1048576], P('vec', 'leaf'), may hold values from -6 to 6
- near_blocks: bfloat16 [4096, 2, 256, 256], P(('leaf', 'vec')), may hold values from -0.25 to 0.25
- near_list: int32 [4096, 2], P(('leaf', 'vec')), may hold values from 0 to 4095, as said below
- bases: bfloat16 [4096, 256, 64], P(('leaf', 'vec')), may hold values from -0.375 to 0.375
- leaf_maps: bfloat16 [4096, 64, 64], P('leaf'), may hold values from -0.25 to 0.25
- far_blocks: bfloat16 [4096, 6, 64, 64], P('leaf'), may hold values from -0.4375 to 0.4375
- far_list: int32 [4096, 6], P('leaf'), may hold values from 0 to 4095, as said below
- far_count: int32 [4096], P('leaf'), may hold values from 1 to 6, as said below
- level_maps: bfloat16 [128, 7, 64, 64], P('leaf'), may hold values from -0.75 to 0.75
- ancestor_coupling_blocks: bfloat16 [128, 7, 64, 64], P('leaf'), may hold values from -0.25 to 0.25
Outputs:
- product: float32 [16, 1048576], P('vec', 'leaf')
Inputs may be any that keep to these rules, and one draw needn't show every extreme that they name: Both column clusters of a leaf's near-field blocks lie in the leaf's own subtree: near_list[l, n] // 32 == l // 32. Every coupling partner lies in the leaf's own subtree or in the subtree just before or after it: far_list[l, f] // 32 differs from l // 32 by at most one. Slots at or beyond far_count are present but unused. `far_count`: used coupling slots of each leaf; some leaf uses all 6.
All inputs are finite; a program needn't handle non-finite values.
Results may differ from a plain program's by a relative error of at most 0.0055.
Values may be sent and summed in bfloat16 or wider, within the bound.
A program may use at most 64 MiB of HBM per device.

v0:
```python
import jax
import jax.numpy as jnp
from jax import lax
from jax.sharding import PartitionSpec as P


def padded(block, sides, width):
    for axis, dim in sides:
        count = lax.axis_size(axis)
        forward = [(i, i + 1) for i in range(count - 1)]
        backward = [(target, source) for source, target in forward]
        low = lax.ppermute(
            lax.slice_in_dim(block, block.shape[dim] - width, None, axis=dim), axis, forward
        )
        high = lax.ppermute(lax.slice_in_dim(block, 0, width, axis=dim), axis, backward)
        block = jnp.concatenate([low, block, high], axis=dim)
    return block


def partner(block, axis, bit):
    count = lax.axis_size(axis)
    route = []
    for low in range(count):
        high = low | 1 << bit
        if high != low and high < count:
            route += [(low, high), (high, low)]
    return lax.ppermute(block, axis, route)


def local(
    vectors,
    near_blocks,
    near_list,
    bases,
    leaf_maps,
    far_blocks,
    far_list,
    far_count,
    level_maps,
    ancestor_coupling_blocks,
):
    vec_count, point_count = vectors.shape
    cluster_pts = bases.shape[1]
    basis_rank = bases.shape[2]
    leaves = point_count // cluster_pts
    device = lax.axis_index("leaf")
    offset = device * leaves
    local_input_vectors = vectors.reshape(vec_count, leaves, cluster_pts)
    gathered = lax.all_gather(vectors, "vec", axis=0, tiled=True).reshape(-1, leaves, cluster_pts)
    picked = gathered[:, near_list - offset]
    partial_value = jnp.einsum(
        "qnab,vqnb->vqa", near_blocks, picked, preferred_element_type=jnp.float32
    )
    every_basis_matrix = lax.all_gather(bases, "vec", axis=0, tiled=True)
    coeffs = jnp.einsum(
        "yot,nyo->ynt", every_basis_matrix, local_input_vectors, preferred_element_type=jnp.float32
    ).astype(jnp.bfloat16)
    flat_coeffs = coeffs.reshape(leaves, vec_count * basis_rank)
    extended = padded(flat_coeffs, (("leaf", 0),), leaves)
    far_slots = far_blocks.shape[1]
    coupled = extended[far_list - offset + leaves].reshape(leaves, far_slots, vec_count, basis_rank)
    live_slot = jnp.arange(far_slots)[None, :] < far_count[:, None]
    masked = jnp.where(live_slot[:, :, None, None], coupled, jnp.zeros_like(coupled))
    distant_interaction = jnp.einsum(
        "lfab,lfvb->lva", far_blocks, masked, preferred_element_type=jnp.float32
    )
    root_coef = jnp.einsum(
        "lkj,lvk->vj", leaf_maps, coeffs, preferred_element_type=jnp.float32
    ).astype(jnp.bfloat16)
    levels = level_maps.shape[1]
    scales = 2.0 ** (-0.5 * jnp.arange(levels, dtype=jnp.float32))
    stacked = (
        jnp.einsum("tkj,vk->tvj", level_maps[0], root_coef, preferred_element_type=jnp.float32)
        * scales[:, None, None]
    )
    stacked = stacked.reshape(levels, vec_count * basis_rank)
    accrued = stacked
    siblings = []
    for bit_index in range(levels):
        received = partner(accrued, "leaf", bit_index)
        siblings.append(received[bit_index])
        higher = (jnp.arange(levels) > bit_index)[:, None]
        accrued = accrued + jnp.where(higher, received, 0.0)
    sibling_sum = jnp.stack(siblings)
    sib_bf = sibling_sum.reshape(levels, vec_count, basis_rank).astype(jnp.bfloat16)
    coupled_up = jnp.einsum(
        "tkj,tvj->vk", ancestor_coupling_blocks[0], sib_bf, preferred_element_type=jnp.float32
    ).astype(jnp.bfloat16)
    leaf_output_rows = (
        distant_interaction
        + jnp.einsum("lkj,vj->lvk", leaf_maps, coupled_up, preferred_element_type=jnp.float32)
    ).astype(jnp.bfloat16)
    distant_contribution = jnp.einsum(
        "psh,prh->rps", every_basis_matrix, leaf_output_rows, preferred_element_type=jnp.float32
    )
    returned = lax.all_to_all(partial_value, "vec", split_axis=0, concat_axis=1, tiled=True)
    total = returned + distant_contribution
    return total.reshape(vec_count, point_count)


def solution(mesh):
    in_specs = (
        P("vec", "leaf"),
        P(("leaf", "vec"), None, None, None),
        P(("leaf", "vec"), None),
        P(("leaf", "vec"), None, None),
        P("leaf", None, None),
        P("leaf", None, None, None),
        P("leaf", None),
        P("leaf"),
        P("leaf", None, None, None),
        P("leaf", None, None, None),
    )
    out_specs = P("vec", "leaf")
    return jax.shard_map(local, mesh=mesh, in_specs=in_specs, out_specs=out_specs, check_vma=False)
```

profile of v0, /device:TPU:1, one launch (start us, length us, event | category | flops | bytes accessed | tf_op | source)
XLA Modules:
  0.0 109.8 jit_solution(15206495569039523102)
XLA Ops:
  7.3 10.9 %all-gather = bf16[4,4,8192]{2,1,0:T(4,128)(2,1)S(1)} all-gather(bf16[1,4,8192]{2,1,0:T(4,128)(2,1)} %bitcast.75), channel_id=1, replica_groups=mesh['leaf'=128,'vec'=4] {'vec'}, dimensions={0}, use_global_device_ids=true | all-gather | bytes 327680 | tf_op jit(solution)/shard_map/all_gather | solution.py:49
  19.1 1.1 %copy.25 = bf16[16,32,256]{2,0,1:T(8,128)(2,1)S(1)} copy(bf16[16,32,256]{2,1,0:T(8,128)(2,1)} %reshape.70) | data formatting | bytes 524288 | tf_op jit(solution)/shard_map/reshape | solution.py:49
  21.6 2.2 %convolution_bitcast_fusion.1 = f32[16,8,256]{2,0,1:T(8,128)S(1)} fusion(bf16[16,8,2,256]{3,0,2,1:T(8,128)(2,1)S(1)} %bitcast.73, bf16[8,2,256,256]{3,2,1,0:T(8,128)(2,1)} %param.11), kind=kOutput, calls=%fused_computation.4 | convolution fusion | flops 33554432 | bytes 2359296 | tf_op jit(solution)/shard_map/qnab,vqnb->vqa/dot_general | solution.py:51
  24.6 3.4 %all-to-all-start = ((f32[16,8,256]{2,1,0:T(8,128)}), f32[16,8,256]{2,1,0:T(8,128)S(1)}, u32[]{:S(2)}, u32[]{:S(2)}) async-start(f32[16,8,256]{2,1,0:T(8,128)} %copy.26), calls=%async_computation | async-start | bytes 262144 | tf_op jit(solution)/shard_map/all_to_all | solution.py:96
  28.3 15.4 %all-gather.3.cloned.1.call-done = bf16[32,256,64]{1,2,0:T(8,128)(2,1)} async-done(((bf16[8,256,64]{1,2,0:T(8,128)(2,1)}), bf16[32,256,64]{1,2,0:T(8,128)(2,1)}) %all-gather.3.cloned.1.call-update) | async-done | bytes 1048592 | tf_op jit(solution)/shard_map/all_gather | solution.py:54
  43.7 1.6 %convolution_convert_fusion = bf16[32,4,64]{2,1,0:T(4,128)(2,1)S(1)} fusion(bf16[4,32,256]{2,0,1:T(4,128)(2,1)} %bitcast.76, bf16[32,256,64]{1,2,0:T(8,128)(2,1)} %all-gather.3.cloned.1.call-done), kind=kOutput, calls=%fused_computation.9 | convolution fusion | flops 4202496 | bytes 1130496 | tf_op jit(solution)/shard_map/yot,nyo->ynt/dot_general | solution.py:55
  45.4 1.4 %fusion.3 = f32[7,4,64]{2,1,0:T(4,128)S(1)} fusion(bf16[32,4,64]{2,1,0:T(4,128)(2,1)S(1)} %convolution_convert_fusion, bf16[32,64,64]{2,1,0:T(8,128)(2,1)} %param.14, bf16[1,7,64,64]{3,2,1,0:T(8,128)(2,1)} %param.18, f32[7]{0:T(128)S(1)} %multiply_power_fusion), kind=kOutput, calls=%fused_computation.11 | convolution fusion | flops 1280000 | bytes 343068 | tf_op jit(solution)/shard_map/tkj,vk->tvj/dot_general | solution.py:73
  46.9 3.4 %collective-permute-start.2 = (f32[7,256]{1,0:T(8,128)S(1)}, f32[7,256]{1,0:T(8,128)S(1)}, u32[]{:S(2)}, u32[]{:S(2)}) collective-permute-start(f32[7,256]{1,0:T(8,128)S(1)} %reshape.74), channel_id=1, source_target_pairs={{0,4},{4,0},{8,12},{12,8},{16,20},{20,16},{24,28},{28,24},{32,36},... | collective-permute-start | bytes 21512 | tf_op jit(solution)/shard_map/ppermute | solution.py:27
  51.2 2.8 %collective-permute-start.3 = (f32[7,256]{1,0:T(8,128)S(1)}, f32[7,256]{1,0:T(8,128)S(1)}, u32[]{:S(2)}, u32[]{:S(2)}) collective-permute-start(f32[7,256]{1,0:T(8,128)S(1)} %select_add_fusion.5), channel_id=1, source_target_pairs={{0,8},{8,0},{4,12},{12,4},{16,24},{24,16},{20,28},{28,20},{32,40},... | collective-permute-start | bytes 21512 | tf_op jit(solution)/shard_map/ppermute | solution.py:27
  54.0 1.6 %collective-permute-done.3 = f32[7,256]{1,0:T(8,128)S(1)} collective-permute-done((f32[7,256]{1,0:T(8,128)S(1)}, f32[7,256]{1,0:T(8,128)S(1)}, u32[]{:S(2)}, u32[]{:S(2)}) %collective-permute-start.3) | collective-permute-done | bytes 7200 | tf_op jit(solution)/shard_map/ppermute | solution.py:27
  55.6 3.7 %collective-permute-start.4 = (f32[7,256]{1,0:T(8,128)S(1)}, f32[7,256]{1,0:T(8,128)S(1)}, u32[]{:S(2)}, u32[]{:S(2)}) collective-permute-start(f32[7,256]{1,0:T(8,128)S(1)} %select_add_fusion.4), channel_id=1, source_target_pairs={{0,16},{16,0},{4,20},{20,4},{8,24},{24,8},{12,28},{28,12},{32,48},... | collective-permute-start | bytes 21512 | tf_op jit(solution)/shard_map/ppermute | solution.py:27
  59.3 1.6 %collective-permute-done.4 = f32[7,256]{1,0:T(8,128)S(1)} collective-permute-done((f32[7,256]{1,0:T(8,128)S(1)}, f32[7,256]{1,0:T(8,128)S(1)}, u32[]{:S(2)}, u32[]{:S(2)}) %collective-permute-start.4) | collective-permute-done | bytes 7200 | tf_op jit(solution)/shard_map/ppermute | solution.py:27
  61.0 7.0 %collective-permute-start.5 = (f32[7,256]{1,0:T(8,128)S(1)}, f32[7,256]{1,0:T(8,128)S(1)}, u32[]{:S(2)}, u32[]{:S(2)}) collective-permute-start(f32[7,256]{1,0:T(8,128)S(1)} %select_add_fusion.3), channel_id=1, source_target_pairs={{0,32},{32,0},{4,36},{36,4},{8,40},{40,8},{12,44},{44,12},{16,48},... | collective-permute-start | bytes 21512 | tf_op jit(solution)/shard_map/ppermute | solution.py:27
  68.0 1.3 %collective-permute-done.5 = f32[7,256]{1,0:T(8,128)S(1)} collective-permute-done((f32[7,256]{1,0:T(8,128)S(1)}, f32[7,256]{1,0:T(8,128)S(1)}, u32[]{:S(2)}, u32[]{:S(2)}) %collective-permute-start.5) | collective-permute-done | bytes 7200 | tf_op jit(solution)/shard_map/ppermute | solution.py:27
  69.3 3.3 %collective-permute-start.6 = (f32[7,256]{1,0:T(8,128)S(1)}, f32[7,256]{1,0:T(8,128)S(1)}, u32[]{:S(2)}, u32[]{:S(2)}) collective-permute-start(f32[7,256]{1,0:T(8,128)S(1)} %select_add_fusion.2), channel_id=1, source_target_pairs={{0,64},{64,0},{4,68},{68,4},{8,72},{72,8},{12,76},{76,12},{16,80},... | collective-permute-start | bytes 21512 | tf_op jit(solution)/shard_map/ppermute | solution.py:27
  72.6 1.1 %collective-permute-done.6 = f32[7,256]{1,0:T(8,128)S(1)} collective-permute-done((f32[7,256]{1,0:T(8,128)S(1)}, f32[7,256]{1,0:T(8,128)S(1)}, u32[]{:S(2)}, u32[]{:S(2)}) %collective-permute-start.6) | collective-permute-done | bytes 7200 | tf_op jit(solution)/shard_map/ppermute | solution.py:27
  73.8 4.8 %collective-permute-start.7 = (f32[7,256]{1,0:T(8,128)S(1)}, f32[7,256]{1,0:T(8,128)S(1)}, u32[]{:S(2)}, u32[]{:S(2)}) collective-permute-start(f32[7,256]{1,0:T(8,128)S(1)} %select_add_fusion.1), channel_id=1, source_target_pairs={{0,128},{128,0},{4,132},{132,4},{8,136},{136,8},{12,140},{140,12},... | collective-permute-start | bytes 21512 | tf_op jit(solution)/shard_map/ppermute | solution.py:27
  79.4 7.0 %collective-permute-start.1 = (bf16[32,256]{1,0:T(8,128)(2,1)S(1)}, bf16[32,256]{1,0:T(8,128)(2,1)S(1)}, u32[]{:S(2)}, u32[]{:S(2)}) collective-permute-start(bf16[32,256]{1,0:T(8,128)(2,1)S(1)} %reshape.72), channel_id=1, source_target_pairs={{4,0},{8,4},{12,8},{16,12},{20,16},{24,20},{28,24},{32,28},{36,32}... | collective-permute-start | bytes 49160 | tf_op jit(solution)/shard_map/ppermute | solution.py:15
  86.5 3.1 %collective-permute-start = (bf16[32,256]{1,0:T(8,128)(2,1)S(1)}, bf16[32,256]{1,0:T(8,128)(2,1)S(1)}, u32[]{:S(2)}, u32[]{:S(2)}) collective-permute-start(bf16[32,256]{1,0:T(8,128)(2,1)S(1)} %reshape.72), channel_id=1, source_target_pairs={{0,4},{4,8},{8,12},{12,16},{16,20},{20,24},{24,28},{28,32},{32,36}... | collective-permute-start | bytes 49160 | tf_op jit(solution)/shard_map/ppermute | solution.py:12
  89.7 5.6 %collective-permute-start.8 = (bf16[7,256]{1,0:T(8,128)(2,1)S(1)}, bf16[7,256]{1,0:T(8,128)(2,1)S(1)}, u32[]{:S(2)}, u32[]{:S(2)}) collective-permute-start(bf16[7,256]{1,0:T(8,128)(2,1)S(1)} %select_add_fusion), channel_id=1, source_target_pairs={{0,256},{256,0},{4,260},{260,4},{8,264},{264,8},{12,268},{268,12},... | collective-permute-start | bytes 10760 | tf_op jit(solution)/shard_map/ppermute | solution.py:27
  95.3 1.0 gather_fusion.1
  96.5 1.5 %collective-permute-done.8 = bf16[7,256]{1,0:T(8,128)(2,1)S(1)} collective-permute-done((bf16[7,256]{1,0:T(8,128)(2,1)S(1)}, bf16[7,256]{1,0:T(8,128)(2,1)S(1)}, u32[]{:S(2)}, u32[]{:S(2)}) %collective-permute-start.8) | collective-permute-done | bytes 3616 | tf_op jit(solution)/shard_map/ppermute | solution.py:27
  98.1 1.8 %convolution_bitcast_fusion.3 = f32[32,4,64]{2,1,0:T(4,128)S(1)} fusion(bf16[32,64,64]{2,1,0:T(8,128)(2,1)} %param.14, bf16[7,4,64]{2,1,0:T(4,128)(2,1)S(1)} %convert_element_type.18, bf16[1,7,64,64]{3,2,1,0:T(8,128)(2,1)} %param.19), kind=kOutput, calls=%fused_computation.7 | convolution fusion | flops 1278208 | bytes 355840 | tf_op jit(solution)/shard_map/lkj,vj->lvk/dot_general | solution.py:91
  99.9 3.0 %fusion = f32[4,32,256]{2,0,1:T(4,128)} fusion(f32[4,32,256]{2,0,1:T(4,128)} %bitcast.77, bf16[32,256,64]{1,2,0:T(8,128)(2,1)} %all-gather.3.cloned.1.call-done, f32[32,4,64]{2,1,0:T(4,128)S(1)} %convolution_bitcast_fusion.3, bf16[32,6,64,64]{3,2,1,0:T(8,128)(2,1)S(1)} %copy-done, bf16[32,6,4,64]{3,2,1,0:T(4,128)(2,1)S(1)} %reshape.73, ...), kind=kOutput, calls=%fused_computation.3 | convolution fusion | flops 10584064 | bytes 3014848 | tf_op jit(solution)/shard_map/psh,prh->rps/dot_general | solution.py:93
  (52 shorter events, 6.6 us)
Async XLA Ops:
  6.5 93.4 %copy-start = (bf16[32,6,64,64]{3,2,1,0:T(8,128)(2,1)S(1)}, bf16[32,6,64,64]{3,2,1,0:T(8,128)(2,1)}, u32[]{:S(2)}) copy-start(bf16[32,6,64,64]{3,2,1,0:T(8,128)(2,1)} %param.15) | copy-start | bytes 4718596
  6.5 21.4 %copy-start.1 = (s32[32,6]{0,1:T(8,128)S(1)}, s32[32,6]{0,1:T(8,128)}, u32[]{:S(2)}) copy-start(s32[32,6]{0,1:T(8,128)} %param.16) | copy-start | bytes 2308
  6.5 21.7 %copy-start.2 = (s32[32]{0:T(128)S(1)}, s32[32]{0:T(128)}, u32[]{:S(2)}) copy-start(s32[32]{0:T(128)} %param.17) | copy-start | bytes 388
  6.5 37.2 %all-gather.3.cloned.1.call-start = ((), (), s32[]{:S(2)}) async-start(), calls=%async_computation.1 | async-start | bytes 1310720 | tf_op jit(solution)/shard_map/all_gather | solution.py:54
  24.6 54.0 %all-to-all-start = ((f32[16,8,256]{2,1,0:T(8,128)}), f32[16,8,256]{2,1,0:T(8,128)S(1)}, u32[]{:S(2)}, u32[]{:S(2)}) async-start(f32[16,8,256]{2,1,0:T(8,128)} %copy.26), calls=%async_computation | async-start | bytes 262144 | tf_op jit(solution)/shard_map/all_to_all | solution.py:96
  46.9 4.2 %collective-permute-start.2 = (f32[7,256]{1,0:T(8,128)S(1)}, f32[7,256]{1,0:T(8,128)S(1)}, u32[]{:S(2)}, u32[]{:S(2)}) collective-permute-start(f32[7,256]{1,0:T(8,128)S(1)} %reshape.74), channel_id=1, source_target_pairs={{0,4},{4,0},{8,12},{12,8},{16,20},{20,16},{24,28},{28,24},{32,36},... | collective-permute-start | bytes 21512 | tf_op jit(solution)/shard_map/ppermute | solution.py:27
  51.2 4.4 %collective-permute-start.3 = (f32[7,256]{1,0:T(8,128)S(1)}, f32[7,256]{1,0:T(8,128)S(1)}, u32[]{:S(2)}, u32[]{:S(2)}) collective-permute-start(f32[7,256]{1,0:T(8,128)S(1)} %select_add_fusion.5), channel_id=1, source_target_pairs={{0,8},{8,0},{4,12},{12,4},{16,24},{24,16},{20,28},{28,20},{32,40},... | collective-permute-start | bytes 21512 | tf_op jit(solution)/shard_map/ppermute | solution.py:27
  55.6 5.3 %collective-permute-start.4 = (f32[7,256]{1,0:T(8,128)S(1)}, f32[7,256]{1,0:T(8,128)S(1)}, u32[]{:S(2)}, u32[]{:S(2)}) collective-permute-start(f32[7,256]{1,0:T(8,128)S(1)} %select_add_fusion.4), channel_id=1, source_target_pairs={{0,16},{16,0},{4,20},{20,4},{8,24},{24,8},{12,28},{28,12},{32,48},... | collective-permute-start | bytes 21512 | tf_op jit(solution)/shard_map/ppermute | solution.py:27
  61.0 8.3 %collective-permute-start.5 = (f32[7,256]{1,0:T(8,128)S(1)}, f32[7,256]{1,0:T(8,128)S(1)}, u32[]{:S(2)}, u32[]{:S(2)}) collective-permute-start(f32[7,256]{1,0:T(8,128)S(1)} %select_add_fusion.3), channel_id=1, source_target_pairs={{0,32},{32,0},{4,36},{36,4},{8,40},{40,8},{12,44},{44,12},{16,48},... | collective-permute-start | bytes 21512 | tf_op jit(solution)/shard_map/ppermute | solution.py:27
  69.3 4.4 %collective-permute-start.6 = (f32[7,256]{1,0:T(8,128)S(1)}, f32[7,256]{1,0:T(8,128)S(1)}, u32[]{:S(2)}, u32[]{:S(2)}) collective-permute-start(f32[7,256]{1,0:T(8,128)S(1)} %select_add_fusion.2), channel_id=1, source_target_pairs={{0,64},{64,0},{4,68},{68,4},{8,72},{72,8},{12,76},{76,12},{16,80},... | collective-permute-start | bytes 21512 | tf_op jit(solution)/shard_map/ppermute | solution.py:27
  73.8 15.8 %collective-permute-start.7 = (f32[7,256]{1,0:T(8,128)S(1)}, f32[7,256]{1,0:T(8,128)S(1)}, u32[]{:S(2)}, u32[]{:S(2)}) collective-permute-start(f32[7,256]{1,0:T(8,128)S(1)} %select_add_fusion.1), channel_id=1, source_target_pairs={{0,128},{128,0},{4,132},{132,4},{8,136},{136,8},{12,140},{140,12},... | collective-permute-start | bytes 21512 | tf_op jit(solution)/shard_map/ppermute | solution.py:27
  79.4 15.9 %collective-permute-start.1 = (bf16[32,256]{1,0:T(8,128)(2,1)S(1)}, bf16[32,256]{1,0:T(8,128)(2,1)S(1)}, u32[]{:S(2)}, u32[]{:S(2)}) collective-permute-start(bf16[32,256]{1,0:T(8,128)(2,1)S(1)} %reshape.72), channel_id=1, source_target_pairs={{4,0},{8,4},{12,8},{16,12},{20,16},{24,20},{28,24},{32,28},{36,32}... | collective-permute-start | bytes 49160 | tf_op jit(solution)/shard_map/ppermute | solution.py:15
  86.5 8.9 %collective-permute-start = (bf16[32,256]{1,0:T(8,128)(2,1)S(1)}, bf16[32,256]{1,0:T(8,128)(2,1)S(1)}, u32[]{:S(2)}, u32[]{:S(2)}) collective-permute-start(bf16[32,256]{1,0:T(8,128)(2,1)S(1)} %reshape.72), channel_id=1, source_target_pairs={{0,4},{4,8},{8,12},{12,16},{16,20},{20,24},{24,28},{28,32},{32,36}... | collective-permute-start | bytes 49160 | tf_op jit(solution)/shard_map/ppermute | solution.py:12
  89.7 8.3 %collective-permute-start.8 = (bf16[7,256]{1,0:T(8,128)(2,1)S(1)}, bf16[7,256]{1,0:T(8,128)(2,1)S(1)}, u32[]{:S(2)}, u32[]{:S(2)}) collective-permute-start(bf16[7,256]{1,0:T(8,128)(2,1)S(1)} %select_add_fusion), channel_id=1, source_target_pairs={{0,256},{256,0},{4,260},{260,4},{8,264},{264,8},{12,268},{268,12},... | collective-permute-start | bytes 10760 | tf_op jit(solution)/shard_map/ppermute | solution.py:27
Sparse Core Ops, SparseCore 0:
  9.5 34.2 all-gather.2
where the time goes:
time: 110 us
  starting transfers between devices  44 us (40%)
  waiting for transfers between devices  24 us (22%)
  between operations  13.6 us (12%)
  blocking collectives  10.9 us (10%)
  matrix products  10.1 us (9%)
  local copies, waits for them, and re-layouts  5.88 us (5%)
  other arithmetic  1.27 us (1%)
    ppermute x7, starting transfers between devices, partner(): return lax.ppermute(block, axis, route)  30.5 us
    all_gather x1, waiting for transfers between devices, local(): every_basis_matrix = lax.all_gather(bases, 'vec', axis=0, tiled=True)  15.4 us
    all_gather x1, blocking collectives, local(): lax.all_gather(vectors, 'vec', axis=0, tiled=True)  10.9 us
    ppermute x7, waiting for transfers between devices, partner(): return lax.ppermute(block, axis, route)  7.86 us
    ppermute x1, starting transfers between devices, padded(): lax.ppermute(lax.slice_in_dim(block, 0, width, axis=dim), axis, backward)  7.02 us
    all_to_all x1, starting transfers between devices, local(): lax.all_to_all(partial_value, 'vec', split_axis=0, concat_axis=1, tiled=T...  3.4 us
    ppermute x1, starting transfers between devices, padded(): lax.ppermute(lax.slice_in_dim(block, block.shape[dim] - width, None, axis...  3.1 us
    dot_general x1, matrix products, local(): jnp.einsum('psh,prh->rps', every_basis_matrix, leaf_output_rows, preferre...  3.03 us
  transfers between devices with their start and end apart: 11, of which 7 were waited for; matrix products, arithmetic and copies ran while one was open for 11% of the time, Pallas kernels for 0%

commit v1 on v0

v1 whole, which is shorter than its diff:
```python
import functools

import jax
import jax.numpy as jnp
from jax import lax
from jax.experimental import pallas as pl
from jax.experimental.pallas import tpu as pltpu
from jax.sharding import PartitionSpec as P

MESH = pl.DeviceIdType.MESH
F32 = jnp.float32
BF16 = jnp.bfloat16
NN = (((1,), (0,)), ((), ()))
NT = (((1,), (1,)), ((), ()))


def dot(a, b, dims=NN):
    return lax.dot_general(a, b, dims, preferred_element_type=F32)


def drain(ref, sem):
    pltpu.make_async_copy(ref, ref, sem).wait()


def flipped(value, mask, bits):
    out = 0
    for b in range(bits):
        bit = lax.rem(value // (1 << b), 2)
        out = out + (1 << b) * ((1 - bit) if (mask >> b) & 1 else bit)
    return out


def kernel(
    ny,
    nz,
    vectors,
    near_blocks,
    near_list,
    bases,
    leaf_maps,
    far_blocks,
    far_list,
    far_count,
    level_maps,
    coupling,
    out,
    xs,
    x16,
    near_b,
    near_l,
    basis,
    maps,
    far_b,
    far_l,
    far_c,
    level_own,
    level_sib,
    coup,
    roots,
    coefs,
    weights,
    terms,
    tree,
    near_out,
    far_out,
    result,
    loc,
    send,
    recv,
    tree_recv,
    token,
):
    leaf = lax.axis_index("leaf")
    q = lax.axis_index("vec")
    nx = 4
    core = lax.rem(leaf, 2)
    chip = leaf // 2
    y = lax.rem(chip, ny)
    z = chip // ny
    ybits, zbits = ny.bit_length() - 1, nz.bit_length() - 1
    levels = 1 + ybits + zbits

    def leaf_at(zz, yy, cc):
        return (zz * ny + yy) * 2 + cc

    copies = []

    def load(src, dst):
        c = pltpu.make_async_copy(src, dst, loc.at[len(copies)])
        c.start()
        copies.append(c)
        return c

    for g in range(4):
        pltpu.make_async_copy(
            vectors.at[:, pl.ds(g * 2048, 2048)], xs.at[q * 4 + g], loc.at[15]
        ).start()
    l_basis = load(bases, basis)
    l_maps = load(leaf_maps.at[pl.ds(q * 8, 8)], maps)
    l_level = load(level_maps.at[0], level_own)
    l_nl = load(near_list, near_l)
    l_fl = load(far_list, far_l)
    l_fc = load(far_count, far_c)
    l_coup = load(coupling.at[0], coup)
    l_near = load(near_blocks, near_b)
    l_far = load(far_blocks.at[pl.ds(q * 8, 8)], far_b)

    x_peers = [lax.rem(q + d, nx) for d in (1, 2, 3)]
    y_peers = [flipped(y, d, ybits) for d in range(1, ny)]
    z_peers = [flipped(z, d, zbits) for d in range(1, nz)]
    up = lax.rem(leaf + 1, 2 * ny * nz)
    down = lax.rem(leaf + 2 * ny * nz - 1, 2 * ny * nz)
    off_chip = jnp.where(core == 1, up, down)
    sib = leaf_at(z, y, 1 - core)

    near_by = [(leaf, p) for p in x_peers]
    near_by += [(sib, lax.rem(q + d, nx)) for d in range(4)]
    in_plane = [(leaf_at(z, yy, core), q) for yy in y_peers]
    in_plane += [(leaf_at(zz, y, core), q) for zz in z_peers]
    beside = [(off_chip, lax.rem(q + d, nx)) for d in range(4)]

    barrier = pltpu.get_barrier_semaphore()
    first = near_by + in_plane + beside
    for dev in first:
        pl.semaphore_signal(barrier, inc=1, device_id=dev, device_id_type=MESH)
    drain(xs.at[pl.ds(0, 4)], loc.at[15])
    pl.semaphore_wait(barrier, len(first))

    def push(src, dst, k, dev, rsem=None):
        pltpu.make_async_remote_copy(
            src_ref=src,
            dst_ref=dst,
            send_sem=send.at[k],
            recv_sem=recv.at[k] if rsem is None else rsem,
            device_id=dev,
            device_id_type=MESH,
        ).start()

    for p in x_peers:
        push(xs.at[q * 4 + p], xs.at[q * 4 + p], 0, (leaf, p))
    push(level_maps.at[0], level_sib, 1, (sib, q))
    for d in (1, 2, 3):
        for p in x_peers:
            g = lax.rem(p + d, nx)
            push(xs.at[q * 4 + g], xs.at[q * 4 + g], 2, (leaf, p))
    for yy in y_peers:
        pl.semaphore_signal(
            token, inc=1, device_id=(leaf_at(z, yy, core), q), device_id_type=MESH
        )

    def block(g):
        parts = [xs[s * 4 + g].astype(F32) for s in range(4)]
        return jnp.concatenate(parts, axis=0).astype(BF16)

    l_basis.wait()
    l_maps.wait()
    drain(xs.at[pl.ds(0, 3)], recv.at[0])
    own = block(q)
    pairs = []
    for i in range(4):
        two = [
            dot(own[:, (2 * i + j) * 256 : (2 * i + j + 1) * 256], basis[2 * i + j], NT)
            for j in range(2)
        ]
        pairs.append(jnp.concatenate(two, axis=1).astype(BF16))
    part = dot(jnp.concatenate(pairs, axis=1), maps[...].reshape(512, 64))
    roots[q] = part
    for dev in near_by[:3]:
        push(roots.at[q], roots.at[q], 3, dev)
    for dev in near_by[3:]:
        push(roots.at[q], roots.at[4 + q], 3, dev)
    mine = 16 + q * 4
    for i in range(4):
        coefs[mine + i] = pairs[i]
    src = coefs.at[pl.ds(mine, 4)]
    for dev in near_by[:3]:
        push(src, src, 4, dev)
    for d in range(4):
        p = lax.rem(q + d, nx)
        push(src, coefs.at[pl.ds(q * 4, 4)], 4, (up, p))
        push(src, coefs.at[pl.ds(32 + q * 4, 4)], 4, (down, p))

    l_level.wait()
    drain(level_sib, recv.at[1])
    for half, lev in ((0, level_own), (1, level_sib)):
        for i in range(levels // 2):
            t = 1 + 2 * i
            ls = [lev[t]] + ([lev[t + 1]] if t + 1 < levels else [lev[t]])
            weights[half * 64 : half * 64 + 64, i * 128 : i * 128 + 128] = jnp.concatenate(
                ls, axis=1
            )
    drain(xs.at[pl.ds(0, 9)], recv.at[2])
    for g in range(4):
        group = block(g)
        for i in range(8):
            x16[g * 8 + i] = group[:, i * 256 : (i + 1) * 256]

    drain(roots.at[pl.ds(0, 7)], recv.at[3])
    root_own = (roots[0] + roots[1]) + (roots[2] + roots[3])
    root_sib = (roots[4] + roots[5]) + (roots[6] + roots[7])
    root_sib = root_sib.astype(BF16)
    both = jnp.concatenate([root_own.astype(BF16), root_sib], axis=1)
    sums = dot(both, weights[...])
    for t in range(1, levels):
        term = sums[:, (t - 1) * 64 : t * 64] * (2.0 ** (-0.5 * t))
        terms[t - 1] = jnp.concatenate([term[0:8], term[8:16]], axis=1).astype(BF16)
    if ny > 1:
        pl.semaphore_wait(token, ny - 1)
    for d in range(ny * nz - 1, 0, -1):
        t = d.bit_length()
        zz = flipped(z, d // ny, zbits)
        yy = flipped(y, d % ny, ybits)
        push(
            terms.at[t - 1], tree.at[d], 5, (leaf_at(zz, yy, core), q), tree_recv.at[t - 1]
        )

    l_coup.wait()
    level0 = dot(root_sib, level_sib[0])
    coupled = dot(level0.astype(BF16), coup[0], NT)
    l_nl.wait()
    l_near.wait()
    for i in range(8):
        total = None
        for n in range(2):
            at = jnp.clip(near_l[n, i] - leaf * 32, 0, 31)
            one = dot(x16[at], near_b[i, n], NT)
            total = one if total is None else total + one
        near_out[:, i * 256 : (i + 1) * 256] = total
    l_fl.wait()
    l_fc.wait()
    l_far.wait()
    drain(coefs.at[pl.ds(0, 44)], recv.at[4])
    for i in range(8):
        total = None
        for f in range(6):
            at = jnp.clip(far_l[f, q * 8 + i] - leaf * 32 + 32, 0, 95)
            pair = coefs[at // 2].astype(F32)
            odd = jnp.full((16, 64), lax.rem(at, 2), jnp.int32) == 1
            used = jnp.full((16, 64), far_c[q * 8 + i], jnp.int32) > f
            value = jnp.where(odd, pair[:, 64:], pair[:, :64])
            value = jnp.where(used, value, 0.0).astype(BF16)
            one = dot(value, far_b[i, f], NT)
            total = one if total is None else total + one
        far_out[:, i * 64 : (i + 1) * 64] = total

    for t in range(1, levels):
        lo, hi = 1 << (t - 1), 1 << t
        drain(tree.at[pl.ds(lo, hi - lo)], tree_recv.at[t - 1])
        acc = tree[lo].astype(F32)
        for d in range(lo + 1, hi):
            acc = acc + tree[d].astype(F32)
        sibling = jnp.concatenate([acc[:, :64], acc[:, 64:]], axis=0).astype(BF16)
        coupled = coupled + dot(sibling, coup[t], NT)
    lifted = dot(coupled.astype(BF16), maps[...].reshape(512, 64), NT)
    leaf_out = (far_out[...] + lifted).astype(BF16)
    for i in range(8):
        far = dot(leaf_out[:, i * 64 : (i + 1) * 64], basis[i])
        total = far + near_out[:, i * 256 : (i + 1) * 256]
        for p in range(4):
            result[p, :, i * 256 : (i + 1) * 256] = total[4 * p : 4 * p + 4].astype(BF16)
    for p in x_peers:
        push(result.at[p], out.at[q], 6, (leaf, p))
    last = pltpu.make_async_copy(result.at[q], out.at[q], loc.at[14])
    last.start()
    last.wait()
    drain(result.at[pl.ds(0, 3)], recv.at[6])
    drain(xs.at[pl.ds(0, 3)], send.at[0])
    drain(level_sib, send.at[1])
    drain(xs.at[pl.ds(0, 9)], send.at[2])
    drain(roots.at[pl.ds(0, 7)], send.at[3])
    drain(coefs.at[pl.ds(0, 44)], send.at[4])
    drain(tree.at[pl.ds(1, ny * nz - 1)], send.at[5])
    drain(result.at[pl.ds(0, 3)], send.at[6])


def local(
    ny,
    nz,
    vectors,
    near_blocks,
    near_list,
    bases,
    leaf_maps,
    far_blocks,
    far_list,
    far_count,
    level_maps,
    coupling,
):
    levels = level_maps.shape[1]
    anywhere = pl.BlockSpec(memory_space=pl.ANY)
    wide = 128 * (levels // 2)
    gathered = pl.pallas_call(
        functools.partial(kernel, ny, nz),
        out_shape=jax.ShapeDtypeStruct((4, 4, 2048), BF16),
        in_specs=[pl.BlockSpec(memory_space=pltpu.HBM)] * 10,
        out_specs=anywhere,
        scratch_shapes=[
            pltpu.VMEM((16, 4, 2048), BF16),
            pltpu.VMEM((32, 16, 256), BF16),
            pltpu.VMEM((8, 2, 256, 256), BF16),
            pltpu.SMEM((2, 8), jnp.int32),
            pltpu.VMEM((8, 64, 256), BF16),
            pltpu.VMEM((8, 64, 64), BF16),
            pltpu.VMEM((8, 6, 64, 64), BF16),
            pltpu.SMEM((6, 32), jnp.int32),
            pltpu.SMEM((32,), jnp.int32),
            pltpu.VMEM((levels, 64, 64), BF16),
            pltpu.VMEM((levels, 64, 64), BF16),
            pltpu.VMEM((levels, 64, 64), BF16),
            pltpu.VMEM((8, 16, 64), F32),
            pltpu.VMEM((48, 16, 128), BF16),
            pltpu.VMEM((128, wide), BF16),
            pltpu.VMEM((levels - 1, 8, 128), BF16),
            pltpu.VMEM((ny * nz, 8, 128), BF16),
            pltpu.VMEM((16, 2048), F32),
            pltpu.VMEM((16, 512), F32),
            pltpu.VMEM((4, 4, 2048), BF16),
            pltpu.SemaphoreType.DMA((16,)),
            pltpu.SemaphoreType.DMA((7,)),
            pltpu.SemaphoreType.DMA((7,)),
            pltpu.SemaphoreType.DMA((levels - 1,)),
            pltpu.SemaphoreType.REGULAR,
        ],
        compiler_params=pltpu.CompilerParams(
            collective_id=0, has_side_effects=True, vmem_limit_bytes=64 * 2**20
        ),
        name="h2_product",
    )(
        vectors,
        near_blocks,
        near_list.T,
        bases.transpose(0, 2, 1),
        leaf_maps,
        far_blocks,
        far_list.T,
        far_count,
        level_maps,
        coupling,
    )
    return gathered.astype(F32).transpose(1, 0, 2).reshape(4, 8192)


def solution(mesh):
    leaves = mesh.shape["leaf"]
    ny = 8 if leaves == 128 else 2
    nz = leaves // (2 * ny)
    in_specs = (
        P("vec", "leaf"),
        P(("leaf", "vec"), None, None, None),
        P(("leaf", "vec"), None),
        P(("leaf", "vec"), None, None),
        P("leaf", None, None),
        P("leaf", None, None, None),
        P("leaf", None),
        P("leaf"),
        P("leaf", None, None, None),
        P("leaf", None, None, None),
    )
    return jax.shard_map(
        functools.partial(local, ny, nz),
        mesh=mesh,
        in_specs=in_specs,
        out_specs=P("vec", "leaf"),
        check_vma=False,
    )
```

time: 110 us -> 36.7 us (0.33)
  starting transfers between devices: 44 us -> 0 us
  Pallas kernels: 0 us -> 35 us
  waiting for transfers between devices: 24 us -> 0 us
  between operations: 13.6 us -> 0.01 us
  blocking collectives: 10.9 us -> 0 us
  matrix products: 10.1 us -> 0 us
  local copies, waits for them, and re-layouts: 5.88 us -> 0 us
    ppermute x9 -> x0, starting transfers between devices: 40.6 us -> none  [the longest x7 30.5 us: partner(): return lax.ppermute(block, axis, route)]
    pallas_call x0 -> x1, Pallas kernels: none -> 35 us  [local(): pl.pallas_call(functools.partial(kernel, ny, nz), out_shape=jax.ShapeDtyp...]
    all_gather x1 -> x0, waiting for transfers between devices: 15.4 us -> none  [local(): every_basis_matrix = lax.all_gather(bases, 'vec', axis=0, tiled=True)]
    all_gather x1 -> x0, blocking collectives: 10.9 us -> none  [local(): lax.all_gather(vectors, 'vec', axis=0, tiled=True)]
    dot_general x5 -> x0, matrix products: 10.1 us -> none  [the longest x1 3.03 us: local(): jnp.einsum('psh,prh->rps', every_basis_matrix, leaf_output_rows, preferre...]
    ppermute x9 -> x0, waiting for transfers between devices: 7.87 us -> none  [the longest x7 7.86 us: partner(): return lax.ppermute(block, axis, route)]
    all_to_all x1 -> x0, starting transfers between devices: 3.4 us -> none  [local(): lax.all_to_all(partial_value, 'vec', split_axis=0, concat_axis=1, tiled=T...]
    reshape x5 -> x0, local copies, waits for them, and re-layouts: 2.33 us -> none  [the longest x2 2 us: local(): lax.all_gather(vectors, 'vec', axis=0, tiled=True)]
  transfers between devices with their start and end apart: 11 -> 0, of which waited for: 7 -> 0; matrix products, arithmetic and copies ran while one was open for 11% -> 0% of each run, Pallas kernels for 0% -> 0%
where the time goes in v1:
time: 36.7 us; the launch traced here: 36.5 us
  Pallas kernels  35 us (95%)
  other arithmetic  1.5 us (4%)
    pallas_call x1, Pallas kernels, local(): pl.pallas_call(functools.partial(kernel, ny, nz), out_shape=jax.ShapeDtyp...  35 us
    reshape x1, other arithmetic, local(): return gathered.astype(F32).transpose(1, 0, 2).reshape(4, 8192)  1.5 us

profile of v1, /device:TPU:1, one launch (start us, length us, event | category | flops | bytes accessed | tf_op | source)
XLA Modules:
  0.0 36.5 jit_solution(13769767461950896904)
XLA Ops:
  0.0 35.0 %h2_product.1 = bf16[4,4,2048]{2,1,0:T(4,128)(2,1)} custom-call(bf16[4,8192]{1,0:T(4,128)(2,1)} %vectors.1, bf16[8,2,256,256]{3,2,1,0:T(8,128)(2,1)} %near_blocks.1, s32[2,8]{1,0:T(2,128)} %bitcast.8, bf16[8,64,256]{2,1,0:T(8,128)(2,1)} %bitcast.6, bf16[32,64,64]{2,1,0:T(8,128)(2,1)} %leaf_maps.1, bf16[32,6,64,64]{3,2,1,0:T(8,128)(2,1)} %far_blocks.1, ...), custom_call_target="tpu_custom_call" | custom-call | tf_op jit(solution)/shard_map/h2_product/pallas_call | solution.py:293
  35.0 1.5 %reshape.10 = f32[4,4,2048]{2,1,0:T(4,128)} convert(bf16[4,4,2048]{2,1,0:T(4,128)(2,1)} %h2_product.1) | non-fusion elementwise | flops 32768 | bytes 196608 | tf_op jit(solution)/shard_map/reshape | solution.py:341

commit v2 on v1

v2 whole, which is shorter than its diff:
```python
import functools

import jax
import jax.numpy as jnp
from jax import lax
from jax.experimental import pallas as pl
from jax.experimental.pallas import tpu as pltpu
from jax.sharding import PartitionSpec as P

MESH = pl.DeviceIdType.MESH
F32 = jnp.float32
BF16 = jnp.bfloat16
NN = (((1,), (0,)), ((), ()))
NT = (((1,), (1,)), ((), ()))
TN = (((0,), (0,)), ((), ()))
NX, NY, NZ = 4, 8, 8
LEVELS = 7


def dot(a, b, dims=NN):
    return lax.dot_general(a, b, dims, preferred_element_type=F32)


def drain(ref, sem):
    pltpu.make_async_copy(ref, ref, sem).wait()


def flipped(value, mask):
    out = 0
    for b in range(3):
        bit = lax.rem(value // (1 << b), 2)
        out = out + (1 << b) * ((1 - bit) if (mask >> b) & 1 else bit)
    return out


def twice(block):
    zero = jnp.zeros_like(block)
    return jnp.concatenate(
        [jnp.concatenate([block, zero], axis=1), jnp.concatenate([zero, block], axis=1)],
        axis=0,
    )


REACH = (0, 1, 2, 3, 4, 3, 2, 3)
FARTHEST_FIRST = sorted(range(1, NY * NZ), key=lambda d: -(REACH[d // NY] + REACH[d % NY]))


def kernel(
    vectors,
    near_blocks,
    near_list,
    bases,
    leaf_maps,
    far_blocks,
    far_list,
    far_count,
    level_maps,
    coupling,
    out,
    xs,
    own_x,
    x16,
    near_b,
    near_l,
    basis,
    maps,
    far_b,
    far_l,
    far_c,
    level_own,
    level_sib,
    coup,
    lift,
    weights,
    pair_coup,
    roots,
    coefs,
    terms,
    tree,
    local_out,
    result,
    loc,
    send,
    recv,
    tree_recv,
    token,
):
    leaf = lax.axis_index("leaf")
    q = lax.axis_index("vec")
    core = lax.rem(leaf, 2)
    chip = leaf // 2
    y = lax.rem(chip, NY)
    z = chip // NY

    def leaf_at(zz, yy, cc):
        return (zz * NY + yy) * 2 + cc

    sib = leaf_at(z, y, 1 - core)
    up = lax.rem(leaf + 1, 2 * NY * NZ)
    down = lax.rem(leaf + 2 * NY * NZ - 1, 2 * NY * NZ)
    x_peers = [lax.rem(q + d, NX) for d in (1, 2, 3)]
    by_root = [(leaf, p) for p in x_peers] + [(sib, lax.rem(q + d, NX)) for d in range(4)]
    steps = (1, 2, NY - 2, NY - 1)
    close = [(leaf_at(z, lax.rem(y + d, NY), core), q) for d in steps]
    close += [(leaf_at(lax.rem(z + d, NZ), y, core), q) for d in steps]
    row = [(leaf_at(z, lax.rem(y + d, NY), core), q) for d in range(1, NY)]

    barrier = pltpu.get_barrier_semaphore()
    for dev in by_root + close:
        pl.semaphore_signal(barrier, inc=1, device_id=dev, device_id_type=MESH)

    copies = []

    def load(src, dst):
        c = pltpu.make_async_copy(src, dst, loc.at[len(copies)])
        c.start()
        copies.append(c)
        return c

    l_basis = load(bases, basis)
    l_maps = load(leaf_maps.at[pl.ds(q * 8, 8)], maps)
    for g in range(4):
        pltpu.make_async_copy(
            vectors.at[:, pl.ds(g * 2048, 2048)], xs.at[q * 4 + g], loc.at[15]
        ).start()
    l_level = load(level_maps.at[0], level_own)
    l_coup = load(coupling.at[0], coup)
    l_nl = load(near_list, near_l)
    l_fl = load(far_list, far_l)
    l_fc = load(far_count, far_c)
    l_near = load(near_blocks, near_b)
    l_far = load(far_blocks.at[pl.ds(q * 8, 8)], far_b)

    pl.semaphore_wait(barrier, len(by_root + close))

    def push(src, dst, k, dev, rsem=None):
        pltpu.make_async_remote_copy(
            src_ref=src,
            dst_ref=dst,
            send_sem=send.at[k],
            recv_sem=recv.at[k] if rsem is None else rsem,
            device_id=dev,
            device_id_type=MESH,
        ).start()

    def chunk(g):
        return vectors.at[:, pl.ds(pl.multiple_of(g * 2048, 2048), 2048)]

    for p in x_peers:
        push(chunk(p), xs.at[q * 4 + p], 0, (leaf, p))
    push(level_maps.at[0], level_sib, 1, (sib, q))
    for dev in close:
        pl.semaphore_signal(token.at[0], inc=1, device_id=dev, device_id_type=MESH)

    l_basis.wait()
    l_maps.wait()
    for i in range(8):
        block = dot(maps[i], basis[i], TN).astype(BF16)
        lift[0:64, i * 256 : (i + 1) * 256] = block
        lift[64:128, i * 256 : (i + 1) * 256] = block
    l_level.wait()
    weights[0:128, 0:128] = jnp.zeros((128, 128), BF16)
    for t in range(1, LEVELS):
        weights[0:128, t * 128 : (t + 1) * 128] = twice(level_own[t])
    l_coup.wait()
    for t in range(LEVELS):
        pair_coup[t] = twice(coup[t])
    drain(level_sib, recv.at[1])
    for t in range(LEVELS):
        weights[128:256, t * 128 : (t + 1) * 128] = twice(level_sib[t])
    drain(xs.at[pl.ds(0, 4)], loc.at[15])

    def block_of(g):
        parts = [xs[s * 4 + g].astype(F32) for s in range(4)]
        return jnp.concatenate(parts, axis=0).astype(BF16)

    low = lax.broadcasted_iota(jnp.int32, (8, 128), 1) < 64

    drain(xs.at[pl.ds(0, 3)], recv.at[0])
    own = block_of(q)
    part = dot(own, lift[...], NT)
    roots[q] = jnp.where(low, part[0:8], part[8:16])
    for dev in by_root[:3]:
        push(roots.at[q], roots.at[q], 3, dev)
    for dev in by_root[3:]:
        push(roots.at[q], roots.at[4 + q], 3, dev)
    pl.semaphore_wait(token.at[0], len(close))
    for dev in row:
        pl.semaphore_signal(token.at[1], inc=1, device_id=dev, device_id_type=MESH)
    for d in (1, 2, 3):
        for p in x_peers:
            g = lax.rem(p + d, NX)
            push(chunk(g), xs.at[q * 4 + g], 2, (leaf, p))

    own_x[...] = own
    mine = 16 + q * 4
    for i in range(4):
        two = [
            dot(own_x[:, l * 256 : (l + 1) * 256], basis[l], NT) for l in (2 * i, 2 * i + 1)
        ]
        coefs[mine + i] = jnp.concatenate(two, axis=1).astype(BF16)

    drain(roots.at[pl.ds(0, 7)], recv.at[3])
    root_own = (roots[0] + roots[1]) + (roots[2] + roots[3])
    root_sib = (roots[4] + roots[5]) + (roots[6] + roots[7])
    both = jnp.concatenate([root_own, root_sib], axis=1).astype(BF16)
    sums = dot(both, weights[...])
    for t in range(1, LEVELS):
        term = sums[:, t * 128 : (t + 1) * 128] * (2.0 ** (-0.5 * t))
        terms[t - 1] = term.astype(BF16)
    pl.semaphore_wait(token.at[1], len(row))
    for d in FARTHEST_FIRST:
        t = d.bit_length()
        dev = (leaf_at(flipped(z, d // NY), flipped(y, d % NY), core), q)
        push(terms.at[t - 1], tree.at[d], 5, dev, tree_recv.at[t - 1])
    src = coefs.at[pl.ds(mine, 4)]
    for dev in by_root[:3]:
        push(src, src, 4, dev)
    for d in range(4):
        p = lax.rem(q + d, NX)
        push(src, coefs.at[pl.ds(q * 4, 4)], 4, (up, p))
        push(src, coefs.at[pl.ds(32 + q * 4, 4)], 4, (down, p))

    coupled = dot(sums[:, 0:128].astype(BF16), pair_coup[0], NT)
    drain(xs.at[pl.ds(0, 9)], recv.at[2])
    for g in range(4):
        group = block_of(g)
        for i in range(8):
            x16[g * 8 + i] = group[:, i * 256 : (i + 1) * 256]
    l_nl.wait()
    l_near.wait()
    for i in range(8):
        total = None
        for n in range(2):
            at = jnp.clip(near_l[n, i] - leaf * 32, 0, 31)
            one = dot(x16[at], near_b[i, n], NT)
            total = one if total is None else total + one
        local_out[:, i * 256 : (i + 1) * 256] = total
    l_fl.wait()
    l_fc.wait()
    l_far.wait()
    drain(coefs.at[pl.ds(0, 44)], recv.at[4])
    for i in range(8):
        total = None
        for f in range(6):
            at = jnp.clip(far_l[f, q * 8 + i] - leaf * 32 + 32, 0, 95)
            pair = coefs[at // 2].astype(F32)
            odd = jnp.full((16, 64), lax.rem(at, 2), jnp.int32) == 1
            used = jnp.full((16, 64), far_c[q * 8 + i], jnp.int32) > f
            value = jnp.where(odd, pair[:, 64:], pair[:, :64])
            value = jnp.where(used, value, 0.0).astype(BF16)
            one = dot(value, far_b[i, f], NT)
            total = one if total is None else total + one
        local_out[:, i * 256 : (i + 1) * 256] += dot(total.astype(BF16), basis[i])

    for t in range(1, LEVELS):
        lo, hi = 1 << (t - 1), 1 << t
        drain(tree.at[pl.ds(lo, hi - lo)], tree_recv.at[t - 1])
        blocks = [tree[d].astype(F32) for d in range(lo, hi)]
        while len(blocks) > 1:
            blocks = [a + b for a, b in zip(blocks[0::2], blocks[1::2])]
        coupled = coupled + dot(blocks[0].astype(BF16), pair_coup[t], NT)
    spread = jnp.concatenate(
        [jnp.where(low, coupled, 0.0), jnp.where(low, 0.0, coupled)], axis=0
    ).astype(BF16)
    for h in range(2):
        cols = slice(h * 1024, (h + 1) * 1024)
        total = dot(spread, lift[:, cols]) + local_out[:, cols]
        for p in range(4):
            result[p, :, cols] = total[4 * p : 4 * p + 4].astype(BF16)
        for p in x_peers:
            push(result.at[p, :, cols], out.at[q, :, cols], 6, (leaf, p))
    last = pltpu.make_async_copy(result.at[q], out.at[q], loc.at[14])
    last.start()
    drain(xs.at[pl.ds(0, 3)], send.at[0])
    drain(level_sib, send.at[1])
    drain(xs.at[pl.ds(0, 9)], send.at[2])
    drain(roots.at[pl.ds(0, 7)], send.at[3])
    drain(coefs.at[pl.ds(0, 44)], send.at[4])
    drain(tree.at[pl.ds(1, NY * NZ - 1)], send.at[5])
    drain(result.at[pl.ds(0, 3)], send.at[6])
    last.wait()
    drain(result.at[pl.ds(0, 3)], recv.at[6])


def local(
    vectors,
    near_blocks,
    near_list,
    bases,
    leaf_maps,
    far_blocks,
    far_list,
    far_count,
    level_maps,
    coupling,
):
    gathered = pl.pallas_call(
        kernel,
        out_shape=jax.ShapeDtypeStruct((4, 4, 2048), BF16),
        in_specs=[pl.BlockSpec(memory_space=pl.ANY)] * 10,
        out_specs=pl.BlockSpec(memory_space=pl.ANY),
        scratch_shapes=[
            pltpu.VMEM((16, 4, 2048), BF16),
            pltpu.VMEM((16, 2048), BF16),
            pltpu.VMEM((32, 16, 256), BF16),
            pltpu.VMEM((8, 2, 256, 256), BF16),
            pltpu.SMEM((2, 8), jnp.int32),
            pltpu.VMEM((8, 64, 256), BF16),
            pltpu.VMEM((8, 64, 64), BF16),
            pltpu.VMEM((8, 6, 64, 64), BF16),
            pltpu.SMEM((6, 32), jnp.int32),
            pltpu.SMEM((32,), jnp.int32),
            pltpu.VMEM((LEVELS, 64, 64), BF16),
            pltpu.VMEM((LEVELS, 64, 64), BF16),
            pltpu.VMEM((LEVELS, 64, 64), BF16),
            pltpu.VMEM((128, 2048), BF16),
            pltpu.VMEM((256, LEVELS * 128), BF16),
            pltpu.VMEM((LEVELS, 128, 128), BF16),
            pltpu.VMEM((8, 8, 128), F32),
            pltpu.VMEM((48, 16, 128), BF16),
            pltpu.VMEM((LEVELS - 1, 8, 128), BF16),
            pltpu.VMEM((NY * NZ, 8, 128), BF16),
            pltpu.VMEM((16, 2048), F32),
            pltpu.VMEM((4, 4, 2048), BF16),
            pltpu.SemaphoreType.DMA((16,)),
            pltpu.SemaphoreType.DMA((7,)),
            pltpu.SemaphoreType.DMA((7,)),
            pltpu.SemaphoreType.DMA((LEVELS - 1,)),
            pltpu.SemaphoreType.REGULAR((2,)),
        ],
        compiler_params=pltpu.CompilerParams(
            collective_id=0, has_side_effects=True, vmem_limit_bytes=64 * 2**20
        ),
        name="h2_product",
    )(
        vectors,
        near_blocks,
        near_list.T,
        bases.transpose(0, 2, 1),
        leaf_maps,
        far_blocks,
        far_list.T,
        far_count,
        level_maps,
        coupling,
    )
    return gathered.astype(F32).transpose(1, 0, 2).reshape(4, 8192)


def solution(mesh):
    in_specs = (
        P("vec", "leaf"),
        P(("leaf", "vec"), None, None, None),
        P(("leaf", "vec"), None),
        P(("leaf", "vec"), None, None),
        P("leaf", None, None),
        P("leaf", None, None, None),
        P("leaf", None),
        P("leaf"),
        P("leaf", None, None, None),
        P("leaf", None, None, None),
    )
    return jax.shard_map(
        local, mesh=mesh, in_specs=in_specs, out_specs=P("vec", "leaf"), check_vma=False
    )
```

time: 36.7 us -> 35.4 us (0.965)
  the two profiles are of different devices: /device:TPU:1 before, /device:TPU:4 now
where the time goes in v2:
time: 35.4 us; the launch traced here: 35.3 us
  Pallas kernels  33.7 us (95%)
  other arithmetic  1.5 us (4%)
    pallas_call x1, Pallas kernels, local(): pl.pallas_call(kernel, out_shape=jax.ShapeDtypeStruct((4, 4, 2048), BF16)...  33.7 us
    reshape x1, other arithmetic, local(): return gathered.astype(F32).transpose(1, 0, 2).reshape(4, 8192)  1.5 us

profile of v2, /device:TPU:4, one launch (start us, length us, event | category | flops | bytes accessed | tf_op | source)
XLA Modules:
  0.0 35.3 jit_solution(3410073102225942768)
XLA Ops:
  0.0 33.7 %h2_product.1 = bf16[4,4,2048]{2,1,0:T(4,128)(2,1)} custom-call(bf16[4,8192]{1,0:T(4,128)(2,1)} %vectors.1, bf16[8,2,256,256]{3,2,1,0:T(8,128)(2,1)} %near_blocks.1, s32[2,8]{1,0:T(2,128)} %bitcast.8, bf16[8,64,256]{2,1,0:T(8,128)(2,1)} %bitcast.6, bf16[32,64,64]{2,1,0:T(8,128)(2,1)} %leaf_maps.1, bf16[32,6,64,64]{3,2,1,0:T(8,128)(2,1)} %far_blocks.1, ...), custom_call_target="tpu_custom_call" | custom-call | tf_op jit(solution)/shard_map/h2_product/pallas_call | solution.py:298
  33.7 1.5 %reshape.10 = f32[4,4,2048]{2,1,0:T(4,128)} convert(bf16[4,4,2048]{2,1,0:T(4,128)(2,1)} %h2_product.1) | non-fusion elementwise | flops 32768 | bytes 196608 | tf_op jit(solution)/shard_map/reshape | solution.py:348

commit v3 on v2

--- a/solution.py
+++ b/solution.py
@@ -96,13 +96,14 @@
         return (zz * NY + yy) * 2 + cc
 
     sib = leaf_at(z, y, 1 - core)
-    up = lax.rem(leaf + 1, 2 * NY * NZ)
-    down = lax.rem(leaf + 2 * NY * NZ - 1, 2 * NY * NZ)
+    off_chip = lax.rem(leaf + 2 * NY * NZ - 1 + 2 * core, 2 * NY * NZ)
+    off_slot = 32 - 32 * core
     x_peers = [lax.rem(q + d, NX) for d in (1, 2, 3)]
     by_root = [(leaf, p) for p in x_peers] + [(sib, lax.rem(q + d, NX)) for d in range(4)]
     steps = (1, 2, NY - 2, NY - 1)
     close = [(leaf_at(z, lax.rem(y + d, NY), core), q) for d in steps]
     close += [(leaf_at(lax.rem(z + d, NZ), y, core), q) for d in steps]
+    close += [(off_chip, q)]
     row = [(leaf_at(z, lax.rem(y + d, NY), core), q) for d in range(1, NY)]
 
     barrier = pltpu.get_barrier_semaphore()
@@ -144,8 +145,9 @@
         ).start()
 
     def chunk(g):
-        return vectors.at[:, pl.ds(pl.multiple_of(g * 2048, 2048), 2048)]
-
+        return xs.at[q * 4 + g]
+
+    drain(xs.at[pl.ds(0, 4)], loc.at[15])
     for p in x_peers:
         push(chunk(p), xs.at[q * 4 + p], 0, (leaf, p))
     push(level_maps.at[0], level_sib, 1, (sib, q))
@@ -168,7 +170,6 @@
     drain(level_sib, recv.at[1])
     for t in range(LEVELS):
         weights[128:256, t * 128 : (t + 1) * 128] = twice(level_sib[t])
-    drain(xs.at[pl.ds(0, 4)], loc.at[15])
 
     def block_of(g):
         parts = [xs[s * 4 + g].astype(F32) for s in range(4)]
@@ -200,6 +201,14 @@
         ]
         coefs[mine + i] = jnp.concatenate(two, axis=1).astype(BF16)
 
+    src = coefs.at[pl.ds(mine, 4)]
+    for dev in by_root[:3]:
+        push(src, src, 4, dev)
+    for dev in by_root[3:]:
+        push(src, coefs.at[pl.ds(32 - off_slot + q * 4, 4)], 4, dev)
+    for d in range(4):
+        push(src, coefs.at[pl.ds(off_slot + q * 4, 4)], 4, (off_chip, lax.rem(q + d, NX)))
+
     drain(roots.at[pl.ds(0, 7)], recv.at[3])
     root_own = (roots[0] + roots[1]) + (roots[2] + roots[3])
     root_sib = (roots[4] + roots[5]) + (roots[6] + roots[7])
@@ -213,13 +222,6 @@
         t = d.bit_length()
         dev = (leaf_at(flipped(z, d // NY), flipped(y, d % NY), core), q)
         push(terms.at[t - 1], tree.at[d], 5, dev, tree_recv.at[t - 1])
-    src = coefs.at[pl.ds(mine, 4)]
-    for dev in by_root[:3]:
-        push(src, src, 4, dev)
-    for d in range(4):
-        p = lax.rem(q + d, NX)
-        push(src, coefs.at[pl.ds(q * 4, 4)], 4, (up, p))
-        push(src, coefs.at[pl.ds(32 + q * 4, 4)], 4, (down, p))
 
     coupled = dot(sums[:, 0:128].astype(BF16), pair_coup[0], NT)
     drain(xs.at[pl.ds(0, 9)], recv.at[2])
@@ -295,11 +297,23 @@
     level_maps,
     coupling,
 ):
+    operands = (
+        vectors,
+        near_blocks,
+        near_list.T,
+        bases.transpose(0, 2, 1),
+        leaf_maps,
+        far_blocks,
+        far_list.T,
+        far_count,
+        level_maps,
+        coupling,
+    )
     gathered = pl.pallas_call(
         kernel,
-        out_shape=jax.ShapeDtypeStruct((4, 4, 2048), BF16),
+        out_shape=pltpu.VMEM((4, 4, 2048), BF16),
         in_specs=[pl.BlockSpec(memory_space=pl.ANY)] * 10,
-        out_specs=pl.BlockSpec(memory_space=pl.ANY),
+        out_specs=pl.BlockSpec(memory_space=pltpu.VMEM),
         scratch_shapes=[
             pltpu.VMEM((16, 4, 2048), BF16),
             pltpu.VMEM((16, 2048), BF16),
@@ -330,21 +344,10 @@
             pltpu.SemaphoreType.REGULAR((2,)),
         ],
         compiler_params=pltpu.CompilerParams(
-            collective_id=0, has_side_effects=True, vmem_limit_bytes=64 * 2**20
+            collective_id=0, has_side_effects=True, vmem_limit_bytes=48 * 2**20
         ),
         name="h2_product",
-    )(
-        vectors,
-        near_blocks,
-        near_list.T,
-        bases.transpose(0, 2, 1),
-        leaf_maps,
-        far_blocks,
-        far_list.T,
-        far_count,
-        level_maps,
-        coupling,
-    )
+    )(*(pltpu.with_memory_space_constraint(a, pltpu.HBM) for a in operands))
     return gathered.astype(F32).transpose(1, 0, 2).reshape(4, 8192)
 
 

time: 35.4 us -> 33.5 us (0.946)
  the two profiles are of different devices: /device:TPU:4 before, /device:TPU:1 now
where the time goes in v3:
time: 33.5 us; the launch traced here: 33.4 us
  Pallas kernels  32.7 us (98%)
  other arithmetic  0.67 us (2%)
    pallas_call x1, Pallas kernels, local(): pl.pallas_call(kernel, out_shape=pltpu.VMEM((4, 4, 2048), BF16), in_specs...  32.7 us

profile of v3, /device:TPU:1, one launch (start us, length us, event | category | flops | bytes accessed | tf_op | source)
XLA Modules:
  0.0 33.4 jit_solution(16826719012208240810)
XLA Ops:
  0.0 32.7 %h2_product.1 = bf16[4,4,2048]{2,1,0:T(4,128)(2,1)S(1)} custom-call(bf16[4,8192]{1,0:T(4,128)(2,1)} %vectors.1, bf16[8,2,256,256]{3,2,1,0:T(8,128)(2,1)} %near_blocks.1, s32[2,8]{1,0:T(2,128)} %bitcast.8, bf16[8,64,256]{2,1,0:T(8,128)(2,1)} %bitcast.6, bf16[32,64,64]{2,1,0:T(8,128)(2,1)} %leaf_maps.1, bf16[32,6,64,64]{3,2,1,0:T(8,128)(2,1)} %far_blocks.1, ...), custom_call_target="tpu_custom_call" | custom-call | tf_op jit(solution)/shard_map/h2_product/pallas_call | solution.py:312
  32.7 0.7 %reshape.10 = f32[4,4,2048]{2,1,0:T(4,128)} convert(bf16[4,4,2048]{2,1,0:T(4,128)(2,1)S(1)} %h2_product.1) | non-fusion elementwise | flops 32768 | bytes 196608 | tf_op jit(solution)/shard_map/reshape | solution.py:351

commit v4 on v3

--- a/solution.py
+++ b/solution.py
@@ -71,6 +71,7 @@
     level_sib,
     coup,
     lift,
+    lifts,
     weights,
     pair_coup,
     roots,
@@ -79,6 +80,7 @@
     tree,
     local_out,
     result,
+    parts,
     loc,
     send,
     recv,
@@ -96,19 +98,38 @@
         return (zz * NY + yy) * 2 + cc
 
     sib = leaf_at(z, y, 1 - core)
-    off_chip = lax.rem(leaf + 2 * NY * NZ - 1 + 2 * core, 2 * NY * NZ)
+    off_chip = leaf - 1 + 2 * core
     off_slot = 32 - 32 * core
+    has_off = jnp.logical_and(leaf > 0, leaf < 2 * NY * NZ - 1)
     x_peers = [lax.rem(q + d, NX) for d in (1, 2, 3)]
     by_root = [(leaf, p) for p in x_peers] + [(sib, lax.rem(q + d, NX)) for d in range(4)]
     steps = (1, 2, NY - 2, NY - 1)
     close = [(leaf_at(z, lax.rem(y + d, NY), core), q) for d in steps]
-    close += [(leaf_at(lax.rem(z + d, NZ), y, core), q) for d in steps]
-    close += [(off_chip, q)]
+    inside = [
+        (z >= 2, (leaf_at(z - 2, y, core), q)),
+        (z >= 1, (leaf_at(z - 1, y, core), q)),
+        (z < NZ - 1, (leaf_at(z + 1, y, core), q)),
+        (z < NZ - 2, (leaf_at(z + 2, y, core), q)),
+        (has_off, (off_chip, q)),
+    ]
+    n_close = len(close) + sum(jnp.where(ok, 1, 0) for ok, _ in inside)
+    opposite = (leaf_at(lax.rem(z + NZ // 2, NZ), y, core), q)
+    early = z < NZ // 2
     row = [(leaf_at(z, lax.rem(y + d, NY), core), q) for d in range(1, NY)]
 
     barrier = pltpu.get_barrier_semaphore()
-    for dev in by_root + close:
-        pl.semaphore_signal(barrier, inc=1, device_id=dev, device_id_type=MESH)
+
+    def greet(sem, devs):
+        for dev in devs:
+            pl.semaphore_signal(sem, inc=1, device_id=dev, device_id_type=MESH)
+
+    def greet_close(sem):
+        greet(sem, close)
+        for ok, dev in inside:
+            pl.when(ok)(functools.partial(greet, sem, [dev]))
+
+    greet(barrier, by_root)
+    greet_close(barrier)
 
     copies = []
 
@@ -132,7 +153,7 @@
     l_near = load(near_blocks, near_b)
     l_far = load(far_blocks.at[pl.ds(q * 8, 8)], far_b)
 
-    pl.semaphore_wait(barrier, len(by_root + close))
+    pl.semaphore_wait(barrier, len(by_root) + n_close)
 
     def push(src, dst, k, dev, rsem=None):
         pltpu.make_async_remote_copy(
@@ -151,8 +172,7 @@
     for p in x_peers:
         push(chunk(p), xs.at[q * 4 + p], 0, (leaf, p))
     push(level_maps.at[0], level_sib, 1, (sib, q))
-    for dev in close:
-        pl.semaphore_signal(token.at[0], inc=1, device_id=dev, device_id_type=MESH)
+    greet_close(token.at[0])
 
     l_basis.wait()
     l_maps.wait()
@@ -160,6 +180,7 @@
         block = dot(maps[i], basis[i], TN).astype(BF16)
         lift[0:64, i * 256 : (i + 1) * 256] = block
         lift[64:128, i * 256 : (i + 1) * 256] = block
+        lifts[q, :, i * 256 : (i + 1) * 256] = block
     l_level.wait()
     weights[0:128, 0:128] = jnp.zeros((128, 128), BF16)
     for t in range(1, LEVELS):
@@ -175,6 +196,9 @@
         parts = [xs[s * 4 + g].astype(F32) for s in range(4)]
         return jnp.concatenate(parts, axis=0).astype(BF16)
 
+    pl.semaphore_wait(token.at[0], n_close)
+    greet(token.at[1], [opposite])
+
     low = lax.broadcasted_iota(jnp.int32, (8, 128), 1) < 64
 
     drain(xs.at[pl.ds(0, 3)], recv.at[0])
@@ -185,9 +209,6 @@
         push(roots.at[q], roots.at[q], 3, dev)
     for dev in by_root[3:]:
         push(roots.at[q], roots.at[4 + q], 3, dev)
-    pl.semaphore_wait(token.at[0], len(close))
-    for dev in row:
-        pl.semaphore_signal(token.at[1], inc=1, device_id=dev, device_id_type=MESH)
     for d in (1, 2, 3):
         for p in x_peers:
             g = lax.rem(p + d, NX)
@@ -206,8 +227,23 @@
         push(src, src, 4, dev)
     for dev in by_root[3:]:
         push(src, coefs.at[pl.ds(32 - off_slot + q * 4, 4)], 4, dev)
-    for d in range(4):
-        push(src, coefs.at[pl.ds(off_slot + q * 4, 4)], 4, (off_chip, lax.rem(q + d, NX)))
+
+    @pl.when(has_off)
+    def _():
+        for d in range(4):
+            push(src, coefs.at[pl.ds(off_slot + q * 4, 4)], 8, (off_chip, lax.rem(q + d, NX)))
+
+    @pl.when(jnp.logical_not(has_off))
+    def _():
+        coefs[pl.ds(32 * core, 16)] = jnp.zeros((16, 16, 128), BF16)
+
+    def share_lift():
+        for p in x_peers:
+            push(lifts.at[q], lifts.at[q], 6, (leaf, p))
+
+    pl.when(early)(share_lift)
+    pl.semaphore_wait(token.at[1], 1)
+    greet(token.at[2], row)
 
     drain(roots.at[pl.ds(0, 7)], recv.at[3])
     root_own = (roots[0] + roots[1]) + (roots[2] + roots[3])
@@ -217,11 +253,12 @@
     for t in range(1, LEVELS):
         term = sums[:, t * 128 : (t + 1) * 128] * (2.0 ** (-0.5 * t))
         terms[t - 1] = term.astype(BF16)
-    pl.semaphore_wait(token.at[1], len(row))
+    pl.semaphore_wait(token.at[2], len(row))
     for d in FARTHEST_FIRST:
         t = d.bit_length()
         dev = (leaf_at(flipped(z, d // NY), flipped(y, d % NY), core), q)
         push(terms.at[t - 1], tree.at[d], 5, dev, tree_recv.at[t - 1])
+    pl.when(jnp.logical_not(early))(share_lift)
 
     coupled = dot(sums[:, 0:128].astype(BF16), pair_coup[0], NT)
     drain(xs.at[pl.ds(0, 9)], recv.at[2])
@@ -241,7 +278,12 @@
     l_fl.wait()
     l_fc.wait()
     l_far.wait()
-    drain(coefs.at[pl.ds(0, 44)], recv.at[4])
+    drain(coefs.at[pl.ds(0, 28)], recv.at[4])
+
+    @pl.when(has_off)
+    def _():
+        drain(coefs.at[pl.ds(0, 16)], recv.at[8])
+
     for i in range(8):
         total = None
         for f in range(6):
@@ -253,7 +295,13 @@
             value = jnp.where(used, value, 0.0).astype(BF16)
             one = dot(value, far_b[i, f], NT)
             total = one if total is None else total + one
-        local_out[:, i * 256 : (i + 1) * 256] += dot(total.astype(BF16), basis[i])
+        cols = slice(i * 256, (i + 1) * 256)
+        total = local_out[:, cols] + dot(total.astype(BF16), basis[i])
+        for p in range(4):
+            result[p, :, cols] = total[4 * p : 4 * p + 4].astype(BF16)
+    for p in x_peers:
+        push(result.at[p], parts.at[q], 7, (leaf, p))
+    parts[q] = result[q]
 
     for t in range(1, LEVELS):
         lo, hi = 1 << (t - 1), 1 << t
@@ -262,27 +310,28 @@
         while len(blocks) > 1:
             blocks = [a + b for a, b in zip(blocks[0::2], blocks[1::2])]
         coupled = coupled + dot(blocks[0].astype(BF16), pair_coup[t], NT)
-    spread = jnp.concatenate(
-        [jnp.where(low, coupled, 0.0), jnp.where(low, 0.0, coupled)], axis=0
-    ).astype(BF16)
-    for h in range(2):
-        cols = slice(h * 1024, (h + 1) * 1024)
-        total = dot(spread, lift[:, cols]) + local_out[:, cols]
-        for p in range(4):
-            result[p, :, cols] = total[4 * p : 4 * p + 4].astype(BF16)
-        for p in x_peers:
-            push(result.at[p, :, cols], out.at[q, :, cols], 6, (leaf, p))
-    last = pltpu.make_async_copy(result.at[q], out.at[q], loc.at[14])
-    last.start()
+    half = jnp.where(jnp.full((8, 64), q, jnp.int32) < 2, coupled[:, :64], coupled[:, 64:])
+    turned = jnp.concatenate([half[4:8], half[0:4]], axis=0)
+    odd = jnp.full((8, 64), lax.rem(q, 2), jnp.int32) == 1
+    mine4 = jnp.where(odd, turned, half).astype(BF16)
+    drain(lifts.at[pl.ds(0, 3)], recv.at[6])
+    drain(parts.at[pl.ds(0, 3)], recv.at[7])
+    for g in range(4):
+        up_part = dot(mine4, lifts[g])
+        out[:, g * 2048 : (g + 1) * 2048] = up_part[0:4] + parts[g].astype(F32)
     drain(xs.at[pl.ds(0, 3)], send.at[0])
     drain(level_sib, send.at[1])
     drain(xs.at[pl.ds(0, 9)], send.at[2])
     drain(roots.at[pl.ds(0, 7)], send.at[3])
-    drain(coefs.at[pl.ds(0, 44)], send.at[4])
+    drain(coefs.at[pl.ds(0, 28)], send.at[4])
+
+    @pl.when(has_off)
+    def _():
+        drain(coefs.at[pl.ds(0, 16)], send.at[8])
+
     drain(tree.at[pl.ds(1, NY * NZ - 1)], send.at[5])
-    drain(result.at[pl.ds(0, 3)], send.at[6])
-    last.wait()
-    drain(result.at[pl.ds(0, 3)], recv.at[6])
+    drain(lifts.at[pl.ds(0, 3)], send.at[6])
+    drain(parts.at[pl.ds(0, 3)], send.at[7])
 
 
 def local(
@@ -309,9 +358,9 @@
         level_maps,
         coupling,
     )
-    gathered = pl.pallas_call(
+    return pl.pallas_call(
         kernel,
-        out_shape=pltpu.VMEM((4, 4, 2048), BF16),
+        out_shape=pltpu.VMEM((4, 8192), F32),
         in_specs=[pl.BlockSpec(memory_space=pl.ANY)] * 10,
         out_specs=pl.BlockSpec(memory_space=pltpu.VMEM),
         scratch_shapes=[
@@ -329,6 +378,7 @@
             pltpu.VMEM((LEVELS, 64, 64), BF16),
             pltpu.VMEM((LEVELS, 64, 64), BF16),
             pltpu.VMEM((128, 2048), BF16),
+            pltpu.VMEM((4, 64, 2048), BF16),
             pltpu.VMEM((256, LEVELS * 128), BF16),
             pltpu.VMEM((LEVELS, 128, 128), BF16),
             pltpu.VMEM((8, 8, 128), F32),
@@ -337,18 +387,18 @@
             pltpu.VMEM((NY * NZ, 8, 128), BF16),
             pltpu.VMEM((16, 2048), F32),
             pltpu.VMEM((4, 4, 2048), BF16),
+            pltpu.VMEM((4, 4, 2048), BF16),
             pltpu.SemaphoreType.DMA((16,)),
-            pltpu.SemaphoreType.DMA((7,)),
-            pltpu.SemaphoreType.DMA((7,)),
+            pltpu.SemaphoreType.DMA((9,)),
+            pltpu.SemaphoreType.DMA((9,)),
             pltpu.SemaphoreType.DMA((LEVELS - 1,)),
-            pltpu.SemaphoreType.REGULAR((2,)),
+            pltpu.SemaphoreType.REGULAR((3,)),
         ],
         compiler_params=pltpu.CompilerParams(
             collective_id=0, has_side_effects=True, vmem_limit_bytes=48 * 2**20
         ),
         name="h2_product",
     )(*(pltpu.with_memory_space_constraint(a, pltpu.HBM) for a in operands))
-    return gathered.astype(F32).transpose(1, 0, 2).reshape(4, 8192)
 
 
 def solution(mesh):

time: 33.5 us -> 32.6 us (0.973)
  Pallas kernels: 32.7 us -> 31.8 us
  other arithmetic: 0.67 us -> 0 us
  local copies, waits for them, and re-layouts: 0 us -> 0.66 us
    pallas_call x1, Pallas kernels: 32.7 us -> 31.8 us  [local(): pl.pallas_call(kernel, out_shape=pltpu.VMEM((4, 8192), F32), in_specs=[pl...]
    reshape x1 -> x0, other arithmetic: 0.67 us -> none  [local(): return gathered.astype(F32).transpose(1, 0, 2).reshape(4, 8192)]
    unnamed x0 -> x1, local copies, waits for them, and re-layouts: none -> 0.66 us
where the time goes in v4:
time: 32.6 us; the launch traced here: 32.5 us
  Pallas kernels  31.8 us (98%)
  local copies, waits for them, and re-layouts  0.66 us (2%)
    pallas_call x1, Pallas kernels, local(): pl.pallas_call(kernel, out_shape=pltpu.VMEM((4, 8192), F32), in_specs=[pl...  31.8 us
    unnamed x1, local copies, waits for them, and re-layouts  0.66 us

profile of v4, /device:TPU:1, one launch (start us, length us, event | category | flops | bytes accessed | tf_op | source)
XLA Modules:
  0.0 32.5 jit_solution(14948461680974668429)
XLA Ops:
  0.0 31.8 %h2_product.1 = f32[4,8192]{1,0:T(4,128)S(1)} custom-call(bf16[4,8192]{1,0:T(4,128)(2,1)} %vectors.1, bf16[8,2,256,256]{3,2,1,0:T(8,128)(2,1)} %near_blocks.1, s32[2,8]{1,0:T(2,128)} %bitcast.5, bf16[8,64,256]{2,1,0:T(8,128)(2,1)} %bitcast.3, bf16[32,64,64]{2,1,0:T(8,128)(2,1)} %leaf_maps.1, bf16[32,6,64,64]{3,2,1,0:T(8,128)(2,1)} %far_blocks.1, ...), custom_call_target="tpu_custom_call" | custom-call | tf_op jit(solution)/shard_map/h2_product/pallas_call | solution.py:361
  31.8 0.7 %copy.12 = f32[4,8192]{1,0:T(4,128)} copy(f32[4,8192]{1,0:T(4,128)S(1)} %h2_product.1) | data formatting | bytes 262144

commit v5 on v4

--- a/solution.py
+++ b/solution.py
@@ -15,6 +15,7 @@
 TN = (((0,), (0,)), ((), ()))
 NX, NY, NZ = 4, 8, 8
 LEVELS = 7
+EARLY = 3
 
 
 def dot(a, b, dims=NN):
@@ -114,7 +115,8 @@
     ]
     n_close = len(close) + sum(jnp.where(ok, 1, 0) for ok, _ in inside)
     opposite = (leaf_at(lax.rem(z + NZ // 2, NZ), y, core), q)
-    early = z < NZ // 2
+    early = z < EARLY
+    late = jnp.logical_not(early)
     row = [(leaf_at(z, lax.rem(y + d, NY), core), q) for d in range(1, NY)]
 
     barrier = pltpu.get_barrier_semaphore()
@@ -196,9 +198,11 @@
         parts = [xs[s * 4 + g].astype(F32) for s in range(4)]
         return jnp.concatenate(parts, axis=0).astype(BF16)
 
-    pl.semaphore_wait(token.at[0], n_close)
-    greet(token.at[1], [opposite])
-
+    def hear_close():
+        pl.semaphore_wait(token.at[0], n_close)
+        greet(token.at[1], [opposite])
+
+    pl.when(late)(hear_close)
     low = lax.broadcasted_iota(jnp.int32, (8, 128), 1) < 64
 
     drain(xs.at[pl.ds(0, 3)], recv.at[0])
@@ -222,6 +226,7 @@
         ]
         coefs[mine + i] = jnp.concatenate(two, axis=1).astype(BF16)
 
+    pl.when(early)(hear_close)
     src = coefs.at[pl.ds(mine, 4)]
     for dev in by_root[:3]:
         push(src, src, 4, dev)
@@ -237,9 +242,35 @@
     def _():
         coefs[pl.ds(32 * core, 16)] = jnp.zeros((16, 16, 128), BF16)
 
+    right, left = lax.rem(q + 1, NX), lax.rem(q + 3, NX)
+
     def share_lift():
-        for p in x_peers:
-            push(lifts.at[q], lifts.at[q], 6, (leaf, p))
+        push(lifts.at[q], lifts.at[q], 6, (leaf, right))
+        push(lifts.at[q], lifts.at[q], 9, (leaf, left))
+
+    def pass_lift():
+        drain(lifts.at[0], recv.at[6])
+        one = lifts.at[left, pl.ds(0, 32)]
+        push(one, one, 10, (leaf, right))
+        drain(lifts.at[0], recv.at[9])
+        two = lifts.at[right, pl.ds(32, 32)]
+        push(two, two, 11, (leaf, left))
+
+    def near_part():
+        drain(xs.at[pl.ds(0, 9)], recv.at[2])
+        for g in range(4):
+            group = block_of(g)
+            for i in range(8):
+                x16[g * 8 + i] = group[:, i * 256 : (i + 1) * 256]
+        l_nl.wait()
+        l_near.wait()
+        for i in range(8):
+            total = None
+            for n in range(2):
+                at = jnp.clip(near_l[n, i] - leaf * 32, 0, 31)
+                one = dot(x16[at], near_b[i, n], NT)
+                total = one if total is None else total + one
+            local_out[:, i * 256 : (i + 1) * 256] = total
 
     pl.when(early)(share_lift)
     pl.semaphore_wait(token.at[1], 1)
@@ -258,23 +289,10 @@
         t = d.bit_length()
         dev = (leaf_at(flipped(z, d // NY), flipped(y, d % NY), core), q)
         push(terms.at[t - 1], tree.at[d], 5, dev, tree_recv.at[t - 1])
-    pl.when(jnp.logical_not(early))(share_lift)
 
     coupled = dot(sums[:, 0:128].astype(BF16), pair_coup[0], NT)
-    drain(xs.at[pl.ds(0, 9)], recv.at[2])
-    for g in range(4):
-        group = block_of(g)
-        for i in range(8):
-            x16[g * 8 + i] = group[:, i * 256 : (i + 1) * 256]
-    l_nl.wait()
-    l_near.wait()
-    for i in range(8):
-        total = None
-        for n in range(2):
-            at = jnp.clip(near_l[n, i] - leaf * 32, 0, 31)
-            one = dot(x16[at], near_b[i, n], NT)
-            total = one if total is None else total + one
-        local_out[:, i * 256 : (i + 1) * 256] = total
+    pl.when(early)(pass_lift)
+    near_part()
     l_fl.wait()
     l_fc.wait()
     l_far.wait()
@@ -295,13 +313,21 @@
             value = jnp.where(used, value, 0.0).astype(BF16)
             one = dot(value, far_b[i, f], NT)
             total = one if total is None else total + one
-        cols = slice(i * 256, (i + 1) * 256)
-        total = local_out[:, cols] + dot(total.astype(BF16), basis[i])
+        local_out[:, i * 256 : (i + 1) * 256] += dot(total.astype(BF16), basis[i])
+
+    def give_back(total, cols):
         for p in range(4):
             result[p, :, cols] = total[4 * p : 4 * p + 4].astype(BF16)
-    for p in x_peers:
-        push(result.at[p], parts.at[q], 7, (leaf, p))
-    parts[q] = result[q]
+        for p in x_peers:
+            push(result.at[p, :, cols], parts.at[q, :, cols], 7, (leaf, p))
+
+    halves = (slice(0, 1024), slice(1024, 2048))
+
+    @pl.when(early)
+    def _():
+        for cols in halves:
+            give_back(local_out[:, cols], cols)
+        parts[q] = result[q]
 
     for t in range(1, LEVELS):
         lo, hi = 1 << (t - 1), 1 << t
@@ -310,15 +336,37 @@
         while len(blocks) > 1:
             blocks = [a + b for a, b in zip(blocks[0::2], blocks[1::2])]
         coupled = coupled + dot(blocks[0].astype(BF16), pair_coup[t], NT)
-    half = jnp.where(jnp.full((8, 64), q, jnp.int32) < 2, coupled[:, :64], coupled[:, 64:])
-    turned = jnp.concatenate([half[4:8], half[0:4]], axis=0)
-    odd = jnp.full((8, 64), lax.rem(q, 2), jnp.int32) == 1
-    mine4 = jnp.where(odd, turned, half).astype(BF16)
-    drain(lifts.at[pl.ds(0, 3)], recv.at[6])
-    drain(parts.at[pl.ds(0, 3)], recv.at[7])
-    for g in range(4):
-        up_part = dot(mine4, lifts[g])
-        out[:, g * 2048 : (g + 1) * 2048] = up_part[0:4] + parts[g].astype(F32)
+
+    @pl.when(early)
+    def _():
+        right = jnp.full((8, 64), q, jnp.int32) < 2
+        half = jnp.where(right, coupled[:, :64], coupled[:, 64:])
+        turned = jnp.concatenate([half[4:8], half[0:4]], axis=0)
+        odd = jnp.full((8, 64), lax.rem(q, 2), jnp.int32) == 1
+        mine4 = jnp.where(odd, turned, half).astype(BF16)
+        drain(lifts.at[0, pl.ds(0, 32)], recv.at[10])
+        drain(lifts.at[0, pl.ds(0, 32)], recv.at[11])
+        drain(parts.at[pl.ds(0, 3)], recv.at[7])
+        for g in range(4):
+            up_part = dot(mine4, lifts[g])
+            out[:, g * 2048 : (g + 1) * 2048] = up_part[0:4] + parts[g].astype(F32)
+        drain(lifts.at[0], send.at[6])
+        drain(lifts.at[0], send.at[9])
+        drain(lifts.at[0, pl.ds(0, 32)], send.at[10])
+        drain(lifts.at[0, pl.ds(0, 32)], send.at[11])
+
+    @pl.when(late)
+    def _():
+        spread = jnp.concatenate(
+            [jnp.where(low, coupled, 0.0), jnp.where(low, 0.0, coupled)], axis=0
+        ).astype(BF16)
+        for cols in halves:
+            give_back(dot(spread, lift[:, cols]) + local_out[:, cols], cols)
+        parts[q] = result[q]
+        drain(parts.at[pl.ds(0, 3)], recv.at[7])
+        for g in range(4):
+            out[:, g * 2048 : (g + 1) * 2048] = parts[g].astype(F32)
+
     drain(xs.at[pl.ds(0, 3)], send.at[0])
     drain(level_sib, send.at[1])
     drain(xs.at[pl.ds(0, 9)], send.at[2])
@@ -330,7 +378,6 @@
         drain(coefs.at[pl.ds(0, 16)], send.at[8])
 
     drain(tree.at[pl.ds(1, NY * NZ - 1)], send.at[5])
-    drain(lifts.at[pl.ds(0, 3)], send.at[6])
     drain(parts.at[pl.ds(0, 3)], send.at[7])
 
 
@@ -389,8 +436,8 @@
             pltpu.VMEM((4, 4, 2048), BF16),
             pltpu.VMEM((4, 4, 2048), BF16),
             pltpu.SemaphoreType.DMA((16,)),
-            pltpu.SemaphoreType.DMA((9,)),
-            pltpu.SemaphoreType.DMA((9,)),
+            pltpu.SemaphoreType.DMA((12,)),
+            pltpu.SemaphoreType.DMA((12,)),
             pltpu.SemaphoreType.DMA((LEVELS - 1,)),
             pltpu.SemaphoreType.REGULAR((3,)),
         ],

time: 32.6 us -> 30.6 us (0.939)
  Pallas kernels: 31.8 us -> 29.9 us
    pallas_call x1, Pallas kernels: 31.8 us -> 29.9 us  [local(): pl.pallas_call(kernel, out_shape=pltpu.VMEM((4, 8192), F32), in_specs=[pl...]
where the time goes in v5:
time: 30.6 us; the launch traced here: 30.5 us
  Pallas kernels  29.9 us (98%)
  local copies, waits for them, and re-layouts  0.66 us (2%)
    pallas_call x1, Pallas kernels, local(): pl.pallas_call(kernel, out_shape=pltpu.VMEM((4, 8192), F32), in_specs=[pl...  29.9 us
    unnamed x1, local copies, waits for them, and re-layouts  0.66 us

profile of v5, /device:TPU:1, one launch (start us, length us, event | category | flops | bytes accessed | tf_op | source)
XLA Modules:
  0.0 30.5 jit_solution(4985732229333922863)
XLA Ops:
  0.0 29.9 %h2_product.1 = f32[4,8192]{1,0:T(4,128)S(1)} custom-call(bf16[4,8192]{1,0:T(4,128)(2,1)} %vectors.1, bf16[8,2,256,256]{3,2,1,0:T(8,128)(2,1)} %near_blocks.1, s32[2,8]{1,0:T(2,128)} %bitcast.5, bf16[8,64,256]{2,1,0:T(8,128)(2,1)} %bitcast.3, bf16[32,64,64]{2,1,0:T(8,128)(2,1)} %leaf_maps.1, bf16[32,6,64,64]{3,2,1,0:T(8,128)(2,1)} %far_blocks.1, ...), custom_call_target="tpu_custom_call" | custom-call | tf_op jit(solution)/shard_map/h2_product/pallas_call | solution.py:408
  29.9 0.7 %copy.12 = f32[4,8192]{1,0:T(4,128)} copy(f32[4,8192]{1,0:T(4,128)S(1)} %h2_product.1) | data formatting | bytes 262144

commit v6 on v5

--- a/solution.py
+++ b/solution.py
@@ -16,6 +16,7 @@
 NX, NY, NZ = 4, 8, 8
 LEVELS = 7
 EARLY = 3
+SOON = 4
 
 
 def dot(a, b, dims=NN):
@@ -102,8 +103,8 @@
     off_chip = leaf - 1 + 2 * core
     off_slot = 32 - 32 * core
     has_off = jnp.logical_and(leaf > 0, leaf < 2 * NY * NZ - 1)
-    x_peers = [lax.rem(q + d, NX) for d in (1, 2, 3)]
-    by_root = [(leaf, p) for p in x_peers] + [(sib, lax.rem(q + d, NX)) for d in range(4)]
+    x_peers = [lax.rem(q + d, NX) for d in (2, 1, 3)]
+    by_root = [(leaf, p) for p in x_peers] + [(sib, p) for p in x_peers + [q]]
     steps = (1, 2, NY - 2, NY - 1)
     close = [(leaf_at(z, lax.rem(y + d, NY), core), q) for d in steps]
     inside = [
@@ -117,6 +118,7 @@
     opposite = (leaf_at(lax.rem(z + NZ // 2, NZ), y, core), q)
     early = z < EARLY
     late = jnp.logical_not(early)
+    soon = z < SOON
     row = [(leaf_at(z, lax.rem(y + d, NY), core), q) for d in range(1, NY)]
 
     barrier = pltpu.get_barrier_semaphore()
@@ -213,10 +215,13 @@
         push(roots.at[q], roots.at[q], 3, dev)
     for dev in by_root[3:]:
         push(roots.at[q], roots.at[4 + q], 3, dev)
-    for d in (1, 2, 3):
-        for p in x_peers:
-            g = lax.rem(p + d, NX)
-            push(chunk(g), xs.at[q * 4 + g], 2, (leaf, p))
+    def share_rest():
+        for d in (1, 2, 3):
+            for p in x_peers:
+                g = lax.rem(p + d, NX)
+                push(chunk(g), xs.at[q * 4 + g], 2, (leaf, p))
+
+    pl.when(soon)(share_rest)
 
     own_x[...] = own
     mine = 16 + q * 4
@@ -228,15 +233,18 @@
 
     pl.when(early)(hear_close)
     src = coefs.at[pl.ds(mine, 4)]
-    for dev in by_root[:3]:
-        push(src, src, 4, dev)
-    for dev in by_root[3:]:
-        push(src, coefs.at[pl.ds(32 - off_slot + q * 4, 4)], 4, dev)
-
-    @pl.when(has_off)
-    def _():
-        for d in range(4):
-            push(src, coefs.at[pl.ds(off_slot + q * 4, 4)], 8, (off_chip, lax.rem(q + d, NX)))
+    def share_coefs():
+        for dev in by_root[:3]:
+            push(src, src, 4, dev)
+        for dev in by_root[3:]:
+            push(src, coefs.at[pl.ds(32 - off_slot + q * 4, 4)], 4, dev)
+
+        @pl.when(has_off)
+        def _():
+            for d in range(4):
+                push(src, coefs.at[pl.ds(off_slot + q * 4, 4)], 8, (off_chip, lax.rem(q + d, NX)))
+
+    pl.when(soon)(share_coefs)
 
     @pl.when(jnp.logical_not(has_off))
     def _():
@@ -280,15 +288,30 @@
     root_own = (roots[0] + roots[1]) + (roots[2] + roots[3])
     root_sib = (roots[4] + roots[5]) + (roots[6] + roots[7])
     both = jnp.concatenate([root_own, root_sib], axis=1).astype(BF16)
-    sums = dot(both, weights[...])
-    for t in range(1, LEVELS):
-        term = sums[:, t * 128 : (t + 1) * 128] * (2.0 ** (-0.5 * t))
-        terms[t - 1] = term.astype(BF16)
-    pl.semaphore_wait(token.at[2], len(row))
-    for d in FARTHEST_FIRST:
-        t = d.bit_length()
-        dev = (leaf_at(flipped(z, d // NY), flipped(y, d % NY), core), q)
-        push(terms.at[t - 1], tree.at[d], 5, dev, tree_recv.at[t - 1])
+
+    def send_terms(levels):
+        first, width = levels[0] * 128, len(levels) * 128
+        sums = dot(both, weights[:, first : first + width])
+        for i, t in enumerate(levels):
+            if t > 0:
+                term = sums[:, i * 128 : (i + 1) * 128] * (2.0 ** (-0.5 * t))
+                terms[t - 1] = term.astype(BF16)
+        if levels[-1] == LEVELS - 1:
+            pl.semaphore_wait(token.at[2], len(row))
+        for d in FARTHEST_FIRST:
+            t = d.bit_length()
+            if t in levels:
+                dev = (leaf_at(flipped(z, d // NY), flipped(y, d % NY), core), q)
+                push(terms.at[t - 1], tree.at[d], 5, dev, tree_recv.at[t - 1])
+        return sums
+
+    send_terms([LEVELS - 1])
+    sums = send_terms(list(range(LEVELS - 1)))
+
+    @pl.when(jnp.logical_not(soon))
+    def _():
+        share_rest()
+        share_coefs()
 
     coupled = dot(sums[:, 0:128].astype(BF16), pair_coup[0], NT)
     pl.when(early)(pass_lift)

time: 30.6 us -> 29.8 us (0.974)
  Pallas kernels: 29.9 us -> 29.1 us
    pallas_call x1, Pallas kernels: 29.9 us -> 29.1 us  [local(): pl.pallas_call(kernel, out_shape=pltpu.VMEM((4, 8192), F32), in_specs=[pl...]
where the time goes in v6:
time: 29.8 us; the launch traced here: 29.7 us
  Pallas kernels  29.1 us (98%)
  local copies, waits for them, and re-layouts  0.66 us (2%)
    pallas_call x1, Pallas kernels, local(): pl.pallas_call(kernel, out_shape=pltpu.VMEM((4, 8192), F32), in_specs=[pl...  29.1 us
    unnamed x1, local copies, waits for them, and re-layouts  0.66 us

profile of v6, /device:TPU:1, one launch (start us, length us, event | category | flops | bytes accessed | tf_op | source)
XLA Modules:
  0.0 29.7 jit_solution(10117024920267131091)
XLA Ops:
  0.0 29.1 %h2_product.1 = f32[4,8192]{1,0:T(4,128)S(1)} custom-call(bf16[4,8192]{1,0:T(4,128)(2,1)} %vectors.1, bf16[8,2,256,256]{3,2,1,0:T(8,128)(2,1)} %near_blocks.1, s32[2,8]{1,0:T(2,128)} %bitcast.5, bf16[8,64,256]{2,1,0:T(8,128)(2,1)} %bitcast.3, bf16[32,64,64]{2,1,0:T(8,128)(2,1)} %leaf_maps.1, bf16[32,6,64,64]{3,2,1,0:T(8,128)(2,1)} %far_blocks.1, ...), custom_call_target="tpu_custom_call" | custom-call | tf_op jit(solution)/shard_map/h2_product/pallas_call | solution.py:431
  29.1 0.7 %copy.12 = f32[4,8192]{1,0:T(4,128)} copy(f32[4,8192]{1,0:T(4,128)S(1)} %h2_product.1) | data formatting | bytes 262144

commit v7 on v6

--- a/solution.py
+++ b/solution.py
@@ -151,11 +151,6 @@
         ).start()
     l_level = load(level_maps.at[0], level_own)
     l_coup = load(coupling.at[0], coup)
-    l_nl = load(near_list, near_l)
-    l_fl = load(far_list, far_l)
-    l_fc = load(far_count, far_c)
-    l_near = load(near_blocks, near_b)
-    l_far = load(far_blocks.at[pl.ds(q * 8, 8)], far_b)
 
     pl.semaphore_wait(barrier, len(by_root) + n_close)
 
@@ -177,6 +172,11 @@
         push(chunk(p), xs.at[q * 4 + p], 0, (leaf, p))
     push(level_maps.at[0], level_sib, 1, (sib, q))
     greet_close(token.at[0])
+    l_nl = load(near_list, near_l)
+    l_fl = load(far_list, far_l)
+    l_fc = load(far_count, far_c)
+    l_near = load(near_blocks, near_b)
+    l_far = load(far_blocks.at[pl.ds(q * 8, 8)], far_b)
 
     l_basis.wait()
     l_maps.wait()
@@ -354,6 +354,28 @@
 
     for t in range(1, LEVELS):
         lo, hi = 1 << (t - 1), 1 << t
+        if t == LEVELS - 1:
+            drain(xs.at[pl.ds(0, 3)], send.at[0])
+            drain(level_sib, send.at[1])
+            drain(xs.at[pl.ds(0, 9)], send.at[2])
+            drain(roots.at[pl.ds(0, 7)], send.at[3])
+            drain(coefs.at[pl.ds(0, 28)], send.at[4])
+
+            @pl.when(has_off)
+            def _():
+                drain(coefs.at[pl.ds(0, 16)], send.at[8])
+
+            drain(tree.at[pl.ds(1, NY * NZ - 1)], send.at[5])
+
+            @pl.when(early)
+            def _():
+                drain(lifts.at[0], send.at[6])
+                drain(lifts.at[0], send.at[9])
+                drain(lifts.at[0, pl.ds(0, 32)], send.at[10])
+                drain(lifts.at[0, pl.ds(0, 32)], send.at[11])
+                drain(lifts.at[0, pl.ds(0, 32)], recv.at[10])
+                drain(lifts.at[0, pl.ds(0, 32)], recv.at[11])
+
         drain(tree.at[pl.ds(lo, hi - lo)], tree_recv.at[t - 1])
         blocks = [tree[d].astype(F32) for d in range(lo, hi)]
         while len(blocks) > 1:
@@ -367,16 +389,10 @@
         turned = jnp.concatenate([half[4:8], half[0:4]], axis=0)
         odd = jnp.full((8, 64), lax.rem(q, 2), jnp.int32) == 1
         mine4 = jnp.where(odd, turned, half).astype(BF16)
-        drain(lifts.at[0, pl.ds(0, 32)], recv.at[10])
-        drain(lifts.at[0, pl.ds(0, 32)], recv.at[11])
         drain(parts.at[pl.ds(0, 3)], recv.at[7])
         for g in range(4):
             up_part = dot(mine4, lifts[g])
             out[:, g * 2048 : (g + 1) * 2048] = up_part[0:4] + parts[g].astype(F32)
-        drain(lifts.at[0], send.at[6])
-        drain(lifts.at[0], send.at[9])
-        drain(lifts.at[0, pl.ds(0, 32)], send.at[10])
-        drain(lifts.at[0, pl.ds(0, 32)], send.at[11])
 
     @pl.when(late)
     def _():
@@ -389,18 +405,6 @@
         drain(parts.at[pl.ds(0, 3)], recv.at[7])
         for g in range(4):
             out[:, g * 2048 : (g + 1) * 2048] = parts[g].astype(F32)
-
-    drain(xs.at[pl.ds(0, 3)], send.at[0])
-    drain(level_sib, send.at[1])
-    drain(xs.at[pl.ds(0, 9)], send.at[2])
-    drain(roots.at[pl.ds(0, 7)], send.at[3])
-    drain(coefs.at[pl.ds(0, 28)], send.at[4])
-
-    @pl.when(has_off)
-    def _():
-        drain(coefs.at[pl.ds(0, 16)], send.at[8])
-
-    drain(tree.at[pl.ds(1, NY * NZ - 1)], send.at[5])
     drain(parts.at[pl.ds(0, 3)], send.at[7])
 
 

time: 29.8 us -> 29.8 us (level)
  no operation moved by 1% of the time
where the time goes in v7:
time: 29.8 us; the launch traced here: 29.7 us
  Pallas kernels  29 us (97%)
  local copies, waits for them, and re-layouts  0.66 us (2%)
    pallas_call x1, Pallas kernels, local(): pl.pallas_call(kernel, out_shape=pltpu.VMEM((4, 8192), F32), in_specs=[pl...  29 us
    unnamed x1, local copies, waits for them, and re-layouts  0.66 us

profile of v7, /device:TPU:1, one launch (start us, length us, event | category | flops | bytes accessed | tf_op | source)
XLA Modules:
  0.0 29.7 jit_solution(6984810631313986254)
XLA Ops:
  0.0 29.0 %h2_product.1 = f32[4,8192]{1,0:T(4,128)S(1)} custom-call(bf16[4,8192]{1,0:T(4,128)(2,1)} %vectors.1, bf16[8,2,256,256]{3,2,1,0:T(8,128)(2,1)} %near_blocks.1, s32[2,8]{1,0:T(2,128)} %bitcast.5, bf16[8,64,256]{2,1,0:T(8,128)(2,1)} %bitcast.3, bf16[32,64,64]{2,1,0:T(8,128)(2,1)} %leaf_maps.1, bf16[32,6,64,64]{3,2,1,0:T(8,128)(2,1)} %far_blocks.1, ...), custom_call_target="tpu_custom_call" | custom-call | tf_op jit(solution)/shard_map/h2_product/pallas_call | solution.py:435
  29.0 0.7 %copy.12 = f32[4,8192]{1,0:T(4,128)} copy(f32[4,8192]{1,0:T(4,128)S(1)} %h2_product.1) | data formatting | bytes 262144
